TPU v7x, 32 devices: a whole 2x2x4 slice. The times are simulated.
32 devices in a mesh: rep: 4 (over y, core), shard: 8 (over z, x).
Axes of the slice: x: 2, y: 2, z: 4, core: 2. Of those that a mesh axis runs over, the one named last changes fastest.
Arguments:
- tokens: bfloat16 [32768, 1024], P(('rep', 'shard')), may hold values from -6 to 6
- doc_lengths: int32 [32, 4], P(('rep', 'shard')), may hold values from 1 to 512, 1024 in all within a row
- cotangent: bfloat16 [32768, 1024], P(('rep', 'shard')), may hold values from -6 to 6
- qkv_weight: float32 [1024, 3072], P('shard'), may hold values from -0.125 to 0.125
- qkv_firsts: float32 [1024, 3072], P('shard'), may hold values from -0.00048828125 to 0.00048828125
- qkv_seconds: float32 [1024, 3072], P('shard'), may hold values from 2.0644464e-09 to 3.3348748e-08
- dense_weight: float32 [1024, 1024], P('shard'), may hold values from -0.75 to 0.75
- dense_firsts: float32 [1024, 1024], P('shard'), may hold values from -0.00048828125 to 0.00048828125
- dense_seconds: float32 [1024, 1024], P('shard'), may hold values from 2.0644464e-09 to 3.3348748e-08
- expand_weight: float32 [1024, 4096], P('shard'), may hold values from -0.1875 to 0.1875
- expand_firsts: float32 [1024, 4096], P('shard'), may hold values from -0.00048828125 to 0.00048828125
- expand_seconds: float32 [1024, 4096], P('shard'), may hold values from 2.0644464e-09 to 3.3348748e-08
- shrink_weight: float32 [4096, 1024], P('shard'), may hold values from -0.09375 to 0.09375
- shrink_firsts: float32 [4096, 1024], P('shard'), may hold values from -0.00048828125 to 0.00048828125
- shrink_seconds: float32 [4096, 1024], P('shard'), may hold values from 2.0644464e-09 to 3.3348748e-08
- vectors: float32 [1024, 11], P('shard'), may hold values from -1.5 to 2.64
- vec_firsts: float32 [1024, 11], P('shard'), may hold values from -0.00048828125 to 0.00048828125
- vec_seconds: float32 [1024, 11], P('shard'), may hold values from 2.0644464e-09 to 3.3348748e-08
Outputs:
- out: bfloat16 [32768, 1024], P(('rep', 'shard'))
- grad_in: float32 [32768, 1024], P(('rep', 'shard'))
- qkv_momentum: float32 [1024, 3072], P('shard')
- qkv_variance: float32 [1024, 3072], P('shard')
- qkv_renewed: float32 [1024, 3072], P('shard')
- dense_momentum: float32 [1024, 1024], P('shard')
- dense_variance: float32 [1024, 1024], P('shard')
- dense_renewed: float32 [1024, 1024], P('shard')
- expand_momentum: float32 [1024, 4096], P('shard')
- expand_variance: float32 [1024, 4096], P('shard')
- expand_renewed: float32 [1024, 4096], P('shard')
- shrink_momentum: float32 [4096, 1024], P('shard')
- shrink_variance: float32 [4096, 1024], P('shard')
- shrink_renewed: float32 [4096, 1024], P('shard')
- vec_momentum: float32 [1024, 11], P('shard')
- vec_variance: float32 [1024, 11], P('shard')
- vec_renewed: float32 [1024, 11], P('shard')
- grad_norm: float32 [1], replicated
Inputs may be any that keep to these rules, and one draw needn't show every extreme that they name: `doc_lengths`: row r holds, in order, the lengths of the 4 documents packed into sequence r; each row sums to 1024.
All inputs are finite; a program needn't handle non-finite values.
Results may differ from a plain program's by a relative error of at most 0.02.
Values may be sent and summed in bfloat16 or wider, within the bound.
A program may use at most 384 MiB of HBM per device.

v0:
```python
from functools import partial
import math

import jax
import jax.numpy as jnp
from jax import lax
from jax.sharding import PartitionSpec as P

D = 1024
HEADS = 16
HEAD_DIM = 64
ROTARY = 32
FF = 4096
LEN = 1024
STEP = 10


clip_limit = 1.0
matrix_rate = 0.05
vector_rate = 0.8
decay_rate = 0.1


def shortened(shard):

    def short(part):
        return part.astype(jnp.bfloat16) if part.dtype == jnp.float32 else part

    return jax.tree.map(short, shard)


def doc_layout(lengths_rows):
    ends = jnp.cumsum(lengths_rows, axis=-1)
    places = jnp.arange(LEN, dtype=jnp.int32)
    passed = (places[None, :, None] >= ends[:, None, :]).astype(jnp.int32)
    doc_ids = jnp.sum(passed, axis=-1)
    starts = jnp.sum(passed * lengths_rows[:, None, :], axis=-1)
    return (doc_ids, places[None, :] - starts)


def rotary_tables(positions):
    exponent = jnp.arange(0, ROTARY, 2, dtype=jnp.float32) / ROTARY
    frequency = 10000.0 ** (-exponent)
    angles = positions.astype(jnp.float32)[:, None] * frequency[None, :]
    cosine = jnp.concatenate([jnp.cos(angles), jnp.cos(angles)], axis=-1)[:, None, :]
    sine_part = jnp.concatenate([jnp.sin(angles), jnp.sin(angles)], axis=-1)[:, None, :]
    return (cosine, sine_part)


def rotate(heads, cosine, sine_part):
    half_dim = ROTARY // 2
    turned = heads[..., :ROTARY]
    swapped = jnp.concatenate([-turned[..., half_dim:], turned[..., :half_dim]], axis=-1)
    return jnp.concatenate([turned * cosine + swapped * sine_part, heads[..., ROTARY:]], axis=-1)


def rotate_back(heads, cosine, sine_part):
    half_dim = ROTARY // 2
    turned = heads[..., :ROTARY]
    with_sine = turned * sine_part
    swapped = jnp.concatenate([with_sine[..., half_dim:], -with_sine[..., :half_dim]], axis=-1)
    return jnp.concatenate([turned * cosine + swapped, heads[..., ROTARY:]], axis=-1)


def layer_norm(inputs, ln_gain, ln_shift):
    centered = inputs - jnp.mean(inputs, axis=-1, keepdims=True)
    scaled = centered * lax.rsqrt(jnp.mean(centered * centered, axis=-1, keepdims=True) + 1e-05)
    return scaled * ln_gain + ln_shift


def unpack(table):
    table = table.astype(jnp.float32)
    expand_ratio = FF // D
    return (
        table[:, 0],
        table[:, 1],
        table[:, 2:5].T.reshape(3 * D),
        table[:, 5],
        table[:, 6 : 6 + expand_ratio].T.reshape(FF),
        table[:, 6 + expand_ratio],
    )


def masked_scores(rows_q, seq_keys, seq_docs, first_row, key_stop):
    index_all = jnp.arange(LEN, dtype=jnp.int32)
    scores = jnp.einsum(
        "qhd,khd->hqk", rows_q, seq_keys[:key_stop], preferred_element_type=jnp.float32
    )
    allowed = (seq_docs[first_row:key_stop, None] == seq_docs[None, :key_stop]) & (
        index_all[None, :key_stop] <= index_all[first_row:key_stop, None]
    )
    return jnp.where(allowed[None], scores, -1e30)


def attend_forward(pack):
    seq_queries, seq_keys, seq_values, seq_docs = pack
    block_rows = min(512, LEN)
    pieces, log_sums = ([], [])
    for number in range(LEN // block_rows):
        first_row = number * block_rows
        key_stop = first_row + block_rows
        scores = masked_scores(
            seq_queries[first_row:key_stop], seq_keys, seq_docs, first_row, key_stop
        )
        top_score = jnp.max(scores, axis=-1, keepdims=True)
        weights = jnp.exp(scores - top_score)
        totals = jnp.sum(weights, axis=-1, keepdims=True)
        probs = (weights / totals).astype(jnp.bfloat16)
        pieces.append(
            jnp.einsum(
                "hqk,khd->qhd", probs, seq_values[:key_stop], preferred_element_type=jnp.float32
            )
        )
        log_sums.append(top_score + jnp.log(totals))
    return (jnp.concatenate(pieces, axis=0), jnp.concatenate(log_sums, axis=1))


def attend_backward(pack):
    seq_queries, seq_keys, seq_values, seq_docs, seq_sums, seq_grads = pack
    block_rows = min(512, LEN)
    grad_keys = jnp.zeros(seq_keys.shape, jnp.float32)
    grad_values = jnp.zeros(seq_values.shape, jnp.float32)
    query_parts = []
    for number in range(LEN // block_rows):
        first_row = number * block_rows
        key_stop = first_row + block_rows
        rows_q = seq_queries[first_row:key_stop]
        rows_grad = seq_grads[first_row:key_stop]
        scores = masked_scores(rows_q, seq_keys, seq_docs, first_row, key_stop)
        probs = jnp.exp(scores - seq_sums[:, first_row:key_stop])
        grad_probs = jnp.einsum(
            "qhd,khd->hqk", rows_grad, seq_values[:key_stop], preferred_element_type=jnp.float32
        )
        inner = jnp.sum(probs * grad_probs, axis=-1, keepdims=True)
        grad_scores = (probs * (grad_probs - inner)).astype(jnp.bfloat16)
        query_parts.append(
            jnp.einsum(
                "hqk,khd->qhd", grad_scores, seq_keys[:key_stop], preferred_element_type=jnp.float32
            )
        )
        grad_keys = grad_keys.at[:key_stop].add(
            jnp.einsum("hqk,qhd->khd", grad_scores, rows_q, preferred_element_type=jnp.float32)
        )
        grad_values = grad_values.at[:key_stop].add(
            jnp.einsum(
                "hqk,qhd->khd",
                probs.astype(jnp.bfloat16),
                rows_grad,
                preferred_element_type=jnp.float32,
            )
        )
    return (jnp.concatenate(query_parts, axis=0), grad_keys, grad_values)


def adamw(master, firsts, seconds, gradient, factor, step_rate, decay_amount):
    clipped = gradient * factor
    momentum = 0.9 * firsts + 0.1 * clipped
    variance = 0.95 * seconds + 0.05 * clipped * clipped
    corrected = momentum / (1.0 - 0.9**STEP)
    spread = variance / (1.0 - 0.95**STEP)
    renewed = master - step_rate * (corrected / (jnp.sqrt(spread) + 1e-08) + decay_amount * master)
    return (momentum, variance, renewed)


def body(
    tokens,
    doc_lengths,
    cotangent,
    qkv_weight,
    qkv_firsts,
    qkv_seconds,
    dense_weight,
    dense_firsts,
    dense_seconds,
    expand_weight,
    expand_firsts,
    expand_seconds,
    shrink_weight,
    shrink_firsts,
    shrink_seconds,
    vectors,
    vec_firsts,
    vec_seconds,
):
    masters = (vectors, qkv_weight, dense_weight, expand_weight, shrink_weight)
    shards = tuple((master.astype(jnp.bfloat16) for master in masters))
    table, qkv_full, dense_full, expand_full, shrink_full = jax.tree.map(
        lambda part, own: part.astype(own.dtype),
        lax.all_gather(shortened(shards), "shard", axis=0, tiled=True),
        shards,
    )
    ln_gain, ln_shift, qkv_bias, dense_bias, expand_bias, shrink_bias = unpack(table)
    token_count = tokens.shape[0]
    seq_count = token_count // LEN
    doc_ids, positions = doc_layout(doc_lengths)
    cosine, sine_part = rotary_tables(positions.reshape(token_count))
    inputs = tokens.astype(jnp.float32)
    normed_f, norm_back = jax.vjp(layer_norm, inputs, ln_gain, ln_shift)
    normed = normed_f.astype(jnp.bfloat16)
    mixed = jnp.dot(normed, qkv_full, preferred_element_type=jnp.float32) + qkv_bias
    head_shape = (token_count, HEADS, HEAD_DIM)
    seq_shape = (seq_count, LEN, HEADS, HEAD_DIM)
    queries = (
        (rotate(mixed[:, :D].reshape(head_shape), cosine, sine_part) / math.sqrt(HEAD_DIM))
        .astype(jnp.bfloat16)
        .reshape(seq_shape)
    )
    keys_rot = (
        rotate(mixed[:, D : 2 * D].reshape(head_shape), cosine, sine_part)
        .astype(jnp.bfloat16)
        .reshape(seq_shape)
    )
    values = mixed[:, 2 * D :].astype(jnp.bfloat16).reshape(seq_shape)
    attended, log_sums = lax.map(attend_forward, (queries, keys_rot, values, doc_ids))
    attended = attended.reshape(token_count, D).astype(jnp.bfloat16)
    branch_attn = jnp.dot(attended, dense_full, preferred_element_type=jnp.float32) + dense_bias
    pre_act = jnp.dot(normed, expand_full, preferred_element_type=jnp.float32) + expand_bias
    activated_f, gelu_back = jax.vjp(partial(jax.nn.gelu, approximate=True), pre_act)
    activated = activated_f.astype(jnp.bfloat16)
    branch_mlp = jnp.dot(activated, shrink_full, preferred_element_type=jnp.float32) + shrink_bias
    output = (inputs + branch_attn + branch_mlp).astype(jnp.bfloat16)
    qkv_back, dense_back, expand_back, shrink_back = lax.all_gather(
        shortened(shards[1:]), "shard", axis=0, tiled=True
    )
    grad_shrink = jnp.einsum("tf,td->fd", activated, cotangent, preferred_element_type=jnp.float32)
    grad_dense = jnp.einsum("tc,td->cd", attended, cotangent, preferred_element_type=jnp.float32)
    bias_out_grad = jnp.sum(cotangent, axis=0, dtype=jnp.float32)
    grad_act = jnp.einsum("td,fd->tf", cotangent, shrink_back, preferred_element_type=jnp.float32)
    grad_pre = gelu_back(grad_act)[0].astype(jnp.bfloat16)
    grad_expand = jnp.einsum("tc,tf->cf", normed, grad_pre, preferred_element_type=jnp.float32)
    bias_expand_grad = jnp.sum(grad_pre, axis=0, dtype=jnp.float32)
    grad_attended = jnp.einsum(
        "td,cd->tc", cotangent, dense_back, preferred_element_type=jnp.float32
    ).astype(jnp.bfloat16)
    grad_query, grad_key, grad_value = lax.map(
        attend_backward,
        (queries, keys_rot, values, doc_ids, log_sums, grad_attended.reshape(seq_shape)),
    )
    grad_query = rotate_back(grad_query.reshape(head_shape), cosine, sine_part) / math.sqrt(
        HEAD_DIM
    )
    grad_key = rotate_back(grad_key.reshape(head_shape), cosine, sine_part)
    grad_mixed = jnp.concatenate(
        [
            grad_query.reshape(token_count, D),
            grad_key.reshape(token_count, D),
            grad_value.reshape(token_count, D),
        ],
        axis=1,
    ).astype(jnp.bfloat16)
    grad_qkv = jnp.einsum("tc,tm->cm", normed, grad_mixed, preferred_element_type=jnp.float32)
    bias_qkv_grad = jnp.sum(grad_mixed, axis=0, dtype=jnp.float32)
    grad_normed = jnp.einsum("tm,cm->tc", grad_mixed, qkv_back, preferred_element_type=jnp.float32)
    grad_normed = grad_normed + jnp.einsum(
        "tf,cf->tc", grad_pre, expand_back, preferred_element_type=jnp.float32
    )
    grad_inputs, grad_gain, grad_shift = norm_back(grad_normed)
    grad_in = cotangent.astype(jnp.float32) + grad_inputs
    grad_table = jnp.concatenate(
        [
            grad_gain[None],
            grad_shift[None],
            bias_qkv_grad.reshape(3, D),
            bias_out_grad[None],
            bias_expand_grad.reshape(FF // D, D),
            bias_out_grad[None],
        ],
        axis=0,
    ).T
    local_grads = (grad_table, grad_qkv, grad_dense, grad_expand, grad_shrink)
    owned = (
        lax.psum_scatter(
            local_grads[0].astype(jnp.bfloat16), "shard", scatter_dimension=0, tiled=True
        ).astype(jnp.float32),
        lax.psum_scatter(
            local_grads[1].astype(jnp.bfloat16), "shard", scatter_dimension=0, tiled=True
        ).astype(jnp.float32),
        lax.psum_scatter(
            local_grads[2].astype(jnp.bfloat16), "shard", scatter_dimension=0, tiled=True
        ).astype(jnp.float32),
        lax.psum_scatter(
            local_grads[3].astype(jnp.bfloat16), "shard", scatter_dimension=0, tiled=True
        ).astype(jnp.float32),
        lax.psum_scatter(
            local_grads[4].astype(jnp.bfloat16), "shard", scatter_dimension=0, tiled=True
        ).astype(jnp.float32),
    )
    owned = (
        lax.psum(owned[0].astype(jnp.bfloat16), "rep").astype(jnp.float32),
        lax.psum(owned[1].astype(jnp.bfloat16), "rep").astype(jnp.float32),
        lax.psum(owned[2].astype(jnp.bfloat16), "rep").astype(jnp.float32),
        lax.psum(owned[3].astype(jnp.bfloat16), "rep").astype(jnp.float32),
        lax.psum(owned[4].astype(jnp.bfloat16), "rep").astype(jnp.float32),
    )
    squares = sum((jnp.sum(part_grad * part_grad) for part_grad in owned))
    total_squares = lax.psum(squares, "shard")
    grad_norm = jnp.sqrt(total_squares)
    factor = jnp.minimum(1.0, clip_limit / (grad_norm + 1e-06))
    own_table, own_qkv, own_dense, own_expand, own_shrink = owned
    updates = []
    for master, firsts, seconds, gradient, step_rate, decay_amount in (
        (qkv_weight, qkv_firsts, qkv_seconds, own_qkv, matrix_rate, decay_rate),
        (dense_weight, dense_firsts, dense_seconds, own_dense, matrix_rate, decay_rate),
        (expand_weight, expand_firsts, expand_seconds, own_expand, matrix_rate, decay_rate),
        (shrink_weight, shrink_firsts, shrink_seconds, own_shrink, matrix_rate, decay_rate),
        (vectors, vec_firsts, vec_seconds, own_table, vector_rate, 0.0),
    ):
        updates.extend(adamw(master, firsts, seconds, gradient, factor, step_rate, decay_amount))
    return (output, grad_in) + tuple(updates) + (grad_norm.reshape(1),)


def solution(mesh):
    return jax.shard_map(
        body,
        mesh=mesh,
        in_specs=(
            P(("rep", "shard"), None),
            P(("rep", "shard"), None),
            P(("rep", "shard"), None),
            P("shard", None),
            P("shard", None),
            P("shard", None),
            P("shard", None),
            P("shard", None),
            P("shard", None),
            P("shard", None),
            P("shard", None),
            P("shard", None),
            P("shard", None),
            P("shard", None),
            P("shard", None),
            P("shard", None),
            P("shard", None),
            P("shard", None),
        ),
        out_specs=(
            P(("rep", "shard"), None),
            P(("rep", "shard"), None),
            P("shard", None),
            P("shard", None),
            P("shard", None),
            P("shard", None),
            P("shard", None),
            P("shard", None),
            P("shard", None),
            P("shard", None),
            P("shard", None),
            P("shard", None),
            P("shard", None),
            P("shard", None),
            P("shard", None),
            P("shard", None),
            P("shard", None),
            P(),
        ),
        check_vma=False,
    )
```

profile of v0, /device:TPU:0, one launch (start us, length us, event | category | flops | bytes accessed | tf_op | source)
XLA Modules:
  0.0 1109.5 jit_solution(2872803123674852062)
XLA Ops:
  17.3 28.0 %all_gather.19 = bf16[1024,11]{0,1:T(8,128)(2,1)S(1)} all-gather(bf16[128,11]{0,1:T(8,128)(2,1)S(1)} %convert_element_type.140), channel_id=1, replica_groups=mesh['rep'=4,'shard'=8] {'shard'}, dimensions={0}, use_global_device_ids=true | all-gather | bytes 25344 | tf_op jit(solution)/shard_map/all_gather | solution.py:189
  48.9 14.2 %all-gather.7.cloned.1.call-done = bf16[1024,1024]{1,0:T(8,128)(2,1)} async-done(((bf16[128,1024]{1,0:T(8,128)(2,1)}), bf16[1024,1024]{1,0:T(8,128)(2,1)}) %all-gather.7.cloned.1.call-update) | async-done | bytes 2097168 | tf_op jit(solution)/shard_map/all_gather | solution.py:189
  63.1 4.6 convolution_convert_fusion.4
  69.2 94.2 %all-gather.5.cloned.1.call-done = bf16[1024,3072]{1,0:T(8,128)(2,1)} async-done(((bf16[128,3072]{1,0:T(8,128)(2,1)}), bf16[1024,3072]{1,0:T(8,128)(2,1)}) %all-gather.5.cloned.1.call-update) | async-done | bytes 6291472 | tf_op jit(solution)/shard_map/all_gather | solution.py:189
  163.4 9.2 fusion.119
  173.9 4.2 fusion.113
  178.1 5.4 copy.69
  188.3 5.3 copy.70
  195.5 3.1 slice_negate_fusion.2
  203.0 7.4 select_reduce_fusion.1
  210.5 9.1 fusion.15
  219.6 12.1 %multiply_reduce_fusion.1 = (f32[16,512]{1,0:T(8,128)S(1)}, f32[16,512,512]{1,2,0:T(8,128)}) fusion(f32[16,512,512]{1,2,0:T(8,128)} %get-tuple-element.212, f32[16,512]{1,0:T(8,128)S(1)} %log_add_fusion.1, pred[512,512]{0,1:T(8,128)(4,1)S(1)} %compare_and_fusion, bf16[512,16,64]{0,2,1:T(8,128)(2,1)} %bitcast.86, bf16[512,16,64]{0,2,1:T(8,128)(2,1)} %bitcast.96), kind=kOutput, calls=%fused_computation.20 | convolution fusion | flops 553639936 | bytes 35979264 | tf_op jit(solution)/shard_map/while/body/eval_jaxpr/qhd,khd->hqk/dot_general | solution.py:131
  231.8 12.3 %multiply_convert_fusion.1 = bf16[16,512,512]{1,2,0:T(8,128)(2,1)S(1)} fusion(f32[16,512,512]{1,2,0:T(8,128)} %get-tuple-element.214, f32[16,512,512]{1,2,0:T(8,128)} %get-tuple-element.212, f32[16,512]{1,0:T(8,128)S(1)} %get-tuple-element.213, f32[16,512]{1,0:T(8,128)S(1)} %log_add_fusion.1, pred[512,512]{0,1:T(8,128)(4,1)S(1)} %compare_and_fusion), kind=kLoop, calls=%fused_computation.19 | loop fusion | flops 20971520 | bytes 42270720 | tf_op jit(solution)/shard_map/while/body/eval_jaxpr/convert_element_type | solution.py:135
  244.1 3.3 copy-done
  247.4 4.0 convolution_bitcast_fusion.1
  251.4 13.7 %select_reduce_fusion = (f32[16,512]{1,0:T(8,128)S(1)}, f32[16,512,1024]{2,1,0:T(8,128)}) fusion(pred[512,1024]{1,0:T(8,128)(4,1)S(1)} %fusion.57, bf16[1024,16,32]{0,2,1:T(8,128)(2,1)S(1)} %slice.370, bf16[1024,16,32]{0,2,1:T(8,128)(2,1)S(1)} %get-tuple-element.194, bf16[1024,16,64]{0,2,1:T(8,128)(2,1)S(1)} %copy-done.11), kind=kOutput, calls=%fused_computation.6 | convolution fusion | flops 1094705152 | bytes 37257216 | tf_op jit(solution)/shard_map/while/body/eval_jaxpr/qhd,khd->hqk/dot_general | solution.py:86
  265.1 14.7 %fusion = f32[16,512]{1,0:T(8,128)S(1)} fusion(f32[16,512,1024]{2,1,0:T(8,128)} %get-tuple-element.210, f32[16,512]{1,0:T(8,128)S(1)} %get-tuple-element.209, pred[512,1024]{1,0:T(8,128)(4,1)S(1)} %fusion.57), kind=kLoop, calls=%fused_computation.5 | loop fusion | flops 25157632 | bytes 34144256 | tf_op jit(solution)/shard_map/while/body/eval_jaxpr/reduce_sum | solution.py:107
  279.9 25.1 %multiply_reduce_fusion = (f32[16,512]{1,0:T(8,128)S(1)}, f32[16,512,1024]{2,1,0:T(8,128)}) fusion(f32[16,512,1024]{2,1,0:T(8,128)} %get-tuple-element.210, f32[16,512]{1,0:T(8,128)S(1)} %log_add_fusion, pred[512,1024]{1,0:T(8,128)(4,1)S(1)} %fusion.57, bf16[512,16,64]{0,2,1:T(8,128)(2,1)S(1)} %bitcast.95, bf16[1024,16,64]{0,2,1:T(8,128)(2,1)S(1)} %bitcast.84), kind=kOutput, calls=%fused_computation.1 | convolution fusion | flops 1107288064 | bytes 70844416 | tf_op jit(solution)/shard_map/while/body/eval_jaxpr/qhd,khd->hqk/dot_general | solution.py:131
  304.9 28.3 %multiply_convert_fusion = bf16[16,512,1024]{2,1,0:T(8,128)(2,1)} fusion(f32[16,512,1024]{2,1,0:T(8,128)} %get-tuple-element.216, f32[16,512,1024]{2,1,0:T(8,128)} %get-tuple-element.210, f32[16,512]{1,0:T(8,128)S(1)} %get-tuple-element.215, f32[16,512]{1,0:T(8,128)S(1)} %log_add_fusion, pred[512,1024]{1,0:T(8,128)(4,1)S(1)} %fusion.57), kind=kLoop, calls=%fused_computation | loop fusion | flops 41943040 | bytes 84475904 | tf_op jit(solution)/shard_map/while/body/eval_jaxpr/convert_element_type | solution.py:135
  333.2 9.5 bitcast_add_fusion.1
  345.9 8.3 fusion.68
  354.2 14.6 %fusion.67 = bf16[512,16,64]{0,2,1:T(8,128)(2,1)S(1)} fusion(bf16[1024,16,64]{0,2,1:T(8,128)(2,1)S(1)} %bitcast.85, f32[16,512,1024]{2,1,0:T(8,128)} %get-tuple-element.210, f32[16,512]{1,0:T(8,128)S(1)} %fusion, f32[16,512]{1,0:T(8,128)S(1)} %get-tuple-element.209, pred[512,1024]{1,0:T(8,128)(4,1)S(1)} %fusion.57), kind=kOutput, calls=%fused_computation.125 | convolution fusion | flops 1107820544 | bytes 37289984 | tf_op jit(solution)/shard_map/while/body/eval_jaxpr/hqk,khd->qhd/dot_general | solution.py:110
  372.7 12.7 %convolution_bitcast_fusion = f32[512,16,64]{0,2,1:T(8,128)} fusion(bf16[16,512,1024]{2,1,0:T(8,128)(2,1)} %multiply_convert_fusion, bf16[1024,16,32]{0,2,1:T(8,128)(2,1)S(1)} %copy-done.7, bf16[1024,16,32]{0,2,1:T(8,128)(2,1)} %copy-done.8), kind=kOutput, calls=%fused_computation.115 | convolution fusion | flops 1077936128 | bytes 20971520 | tf_op jit(solution)/shard_map/while/body/eval_jaxpr/hqk,khd->qhd/dot_general | solution.py:137
  391.6 3.7 convolution_convert_fusion.3
  395.2 9.0 fusion.59
  404.4 4.4 maximum_add_fusion
  413.1 17.3 %fusion.41 = bf16[1024,16,64]{0,2,1:T(8,128)(2,1)} fusion(f32[512,16,64]{0,2,1:T(8,128)} %fusion.59, bf16[512,16,64]{0,2,1:T(8,128)(2,1)} %bitcast.94, f32[16,512,1024]{2,1,0:T(8,128)} %get-tuple-element.210, f32[16,512]{1,0:T(8,128)S(1)} %copy-done.43, pred[512,1024]{1,0:T(8,128)(4,1)S(1)} %copy-done.15), kind=kOutput, calls=%fused_computation.70 | convolution fusion | flops 1101004800 | bytes 39354368 | tf_op jit(solution)/shard_map/while/body/eval_jaxpr/hqk,qhd->khd/dot_general | solution.py:145
  430.5 12.7 %convolution_convert_fusion.2 = bf16[1024,3072]{1,0:T(8,128)(2,1)} fusion(bf16[1024,1024]{0,1:T(8,128)(2,1)} %bitcast.98, bf16[1024,1024]{0,1:T(8,128)(2,1)} %bitcast.88, bf16[1024,1024]{0,1:T(8,128)(2,1)} %bitcast.91, bf16[1024,1024]{1,0:T(8,128)(2,1)S(1)} %copy-done.2, f32[1024]{0:T(1024)S(1)} %bitcast.120, f32[1024]{0:T(1024)S(1)} %bitcast.105, ...), kind=kOutput, calls=%fused_computation.48 | convolution fusion | flops 6470762496 | bytes 14696448 | tf_op jit(solution)/shard_map/tc,tm->cm/dot_general | solution.py:251
  444.2 15.6 %fusion.97 = f32[1024,4096]{1,0:T(8,128)} fusion(bf16[1024,4096]{1,0:T(8,128)(2,1)} %all-gather.9.cloned.1.call-done, bf16[1024,1024]{1,0:T(8,128)(2,1)S(1)} %copy-done.2, f32[1024]{0:T(1024)S(1)} %bitcast.121, f32[1024]{0:T(1024)S(1)} %bitcast.106, f32[1024]{0:T(1024)S(1)} %copy-done.49, f32[1024]{0:T(1024)S(1)} %copy-done.47), kind=kOutput, calls=%fused_computation.186 | convolution fusion | flops 8596226048 | bytes 27279360 | tf_op jit(solution)/shard_map/dot_general | solution.py:217
  459.8 18.5 %convolution_convert_fusion = bf16[4096,1024]{1,0:T(8,128)(2,1)} fusion(bf16[1024,1024]{1,0:T(8,128)(2,1)S(1)} %copy-done.21, f32[1024,4096]{1,0:T(8,128)} %fusion.97, f32[4096]{0:T(1024)S(1)} %bitcast.113), kind=kOutput, calls=%fused_computation.36 | convolution fusion | flops 8636071936 | bytes 27279360 | tf_op jit(solution)/shard_map/tf,td->fd/dot_general | solution.py:225
  478.4 26.2 %fusion.111 = (bf16[4096]{0:T(1024)(128)(2,1)S(1)}, bf16[1024,4096]{1,0:T(8,128)(2,1)}) fusion(f32[1024,4096]{1,0:T(8,128)} %fusion.97, f32[4096]{0:T(1024)S(1)} %bitcast.114, bf16[1024,1024]{1,0:T(8,128)(2,1)} %param.32, bf16[4096,1024]{1,0:T(8,128)(2,1)} %all-gather.11.cloned.1.call-done), kind=kOutput, calls=%fused_computation.188 | convolution fusion | flops 8682205184 | bytes 35676160 | tf_op jit(solution)/shard_map/td,fd->tf/dot_general | solution.py:228
  504.5 15.0 %convolution_convert_fusion.1 = bf16[1024,4096]{1,0:T(8,128)(2,1)} fusion(bf16[1024,4096]{1,0:T(8,128)(2,1)} %get-tuple-element.179, bf16[1024,1024]{1,0:T(8,128)(2,1)S(1)} %copy-done.2, f32[1024]{0:T(1024)S(1)} %bitcast.122, f32[1024]{0:T(1024)S(1)} %bitcast.107, f32[1024]{0:T(1024)S(1)} %copy-done.49, f32[1024]{0:T(1024)S(1)} %copy-done.47), kind=kOutput, calls=%fused_computation.37 | convolution fusion | flops 8600420352 | bytes 18890752 | tf_op jit(solution)/shard_map/tc,tf->cf/dot_general | solution.py:230
  521.7 4.8 fusion.92
  526.5 12.1 %fusion.93 = f32[1024,1024]{1,0:T(8,128)} fusion(bf16[1024,3072]{1,0:T(8,128)(2,1)} %all-gather.5.cloned.1.call-done, bf16[1024,1024]{0,1:T(8,128)(2,1)} %bitcast.100, bf16[1024,1024]{0,1:T(8,128)(2,1)} %bitcast.90, bf16[1024,1024]{0,1:T(8,128)(2,1)} %bitcast.93), kind=kOutput, calls=%fused_computation.184 | convolution fusion | flops 6461325312 | bytes 16777216 | tf_op jit(solution)/shard_map/tm,cm->tc/dot_general | solution.py:253
  538.6 15.0 %fusion.100 = (bf16[1024]{0:T(1024)(128)(2,1)S(1)}, f32[1024]{0:T(1024)S(1)}, f32[1024,1024]{1,0:T(8,128)S(1)}) fusion(f32[1024]{0:T(1024)S(1)} %bitcast.108, f32[1024]{0:T(1024)S(1)} %copy-done.47, bf16[1024,1024]{1,0:T(8,128)(2,1)S(1)} %copy-done.2, f32[1024,1024]{1,0:T(8,128)} %fusion.93, bf16[1024,4096]{1,0:T(8,128)(2,1)} %get-tuple-element.179, ...), kind=kOutput, calls=%fused_computation.187 | convolution fusion | flops 8597272576 | bytes 27277312 | tf_op jit(solution)/shard_map/tf,cf->tc/dot_general | solution.py:254
  559.1 6.6 fusion.120
  565.8 39.6 %reduce-scatter.8.cloned.1.call-done = bf16[128,3072]{1,0:T(8,128)(2,1)} async-done(((bf16[1024,3072]{1,0:T(8,128)(2,1)}), bf16[128,3072]{1,0:T(8,128)(2,1)}) %reduce-scatter.8.cloned.1.call-update) | async-done | bytes 786448 | tf_op jit(solution)/shard_map/reduce_scatter | solution.py:275
  605.4 151.8 %reduce-scatter.14.cloned.1.call-done = bf16[512,1024]{1,0:T(8,128)(2,1)} async-done(((bf16[4096,1024]{1,0:T(8,128)(2,1)}), bf16[512,1024]{1,0:T(8,128)(2,1)}) %reduce-scatter.14.cloned.1.call-update) | async-done | bytes 1048592 | tf_op jit(solution)/shard_map/reduce_scatter | solution.py:284
  757.2 152.1 %reduce-scatter.12.cloned.1.call-done = bf16[128,4096]{1,0:T(8,128)(2,1)} async-done(((bf16[1024,4096]{1,0:T(8,128)(2,1)}), bf16[128,4096]{1,0:T(8,128)(2,1)}) %reduce-scatter.12.cloned.1.call-update) | async-done | bytes 1048592 | tf_op jit(solution)/shard_map/reduce_scatter | solution.py:281
  909.3 18.8 %fusion.39 = bf16[1024,1024]{1,0:T(8,128)(2,1)} fusion(bf16[1024,1024]{1,0:T(8,128)(2,1)S(1)} %copy-done.2, f32[1024,1024]{1,0:T(8,128)} %fusion.120, f32[1024]{0:T(1024)S(1)} %bitcast.118, f32[1024]{0:T(1024)S(1)} %bitcast.117, bf16[4096,1024]{1,0:T(8,128)(2,1)} %all-gather.11.cloned.1.call-done, f32[1024,4096]{1,0:T(8,128)} %fusion.97, f32[4096]{0:T(1024)S(1)} %bitcast.115), kind=kOutput, calls=%fused_computation.65 | convolution fusion | flops 8638169088 | bytes 33579008 | tf_op jit(solution)/shard_map/dot_general | solution.py:220
  928.2 45.2 %reduce-scatter.16.cloned.1.call-done = bf16[128,11]{1,0:T(8,128)(2,1)} async-done(((bf16[1024,11]{1,0:T(8,128)(2,1)}), bf16[128,11]{1,0:T(8,128)(2,1)}) %reduce-scatter.16.cloned.1.call-update) | async-done | bytes 2832
  974.2 5.7 psum.43
  980.5 63.4 %all-reduce.5.cloned.1.call-done = (bf16[128,3072]{1,0:T(8,128)(2,1)}, bf16[128,1024]{1,0:T(8,128)(2,1)}, bf16[128,4096]{1,0:T(8,128)(2,1)}, bf16[512,1024]{1,0:T(8,128)(2,1)}) async-done(((bf16[128,3072]{1,0:T(8,128)(2,1)}, bf16[128,1024]{1,0:T(8,128)(2,1)}, bf16[128,4096]{1,0:T(8,128)(2,1)}, bf16[512,1024]{1,0:T(8,128)(2,1)}), (bf16[128,3072]{1,0:T(8,128)(2,1)}, bf16[128,1024]{1,0:T(8,128)(2,1)}, ...) | async-done | bytes 3145744 | tf_op jit(solution)/shard_map/psum | solution.py:290
  1055.8 5.1 add_add_fusion.1
  1060.9 22.2 %psum.47 = f32[]{:T(128)} all-reduce(f32[]{:T(128)S(6)} %add.304), channel_id=1, replica_groups=mesh['rep'=4,'shard'=8] {'shard'}, use_global_device_ids=true, to_apply=%region_33.34 | all-reduce | flops 1 | bytes 8 | tf_op jit(solution)/shard_map/psum | solution.py:296
  1087.2 4.6 multiply_subtract_fusion.2
  1092.0 4.0 multiply_subtract_fusion.1
  1097.4 3.9 multiply_subtract_fusion
  (218 shorter events, 68.5 us)
Async XLA Ops:
  7.2 55.9 %all-gather.7.cloned.1.call-start = ((), (), s32[]{:S(2)}) async-start(), calls=%async_computation.6 | async-start | bytes 2359296 | tf_op jit(solution)/shard_map/all_gather | solution.py:189
  9.0 154.4 %all-gather.5.cloned.1.call-start = ((), (), s32[]{:S(2)}) async-start(), calls=%async_computation.5 | async-start | bytes 7077888 | tf_op jit(solution)/shard_map/all_gather | solution.py:189
  11.5 34.5 %copy-start.1 = (bf16[1024,1024]{1,0:T(8,128)(2,1)S(1)}, bf16[1024,1024]{1,0:T(8,128)(2,1)}, u32[]{:S(2)}) copy-start(bf16[1024,1024]{1,0:T(8,128)(2,1)} %param.30) | copy-start | bytes 6291460
  11.5 432.6 %all-gather.9.cloned.1.call-start = ((), (), s32[]{:S(2)}) async-start(), calls=%async_computation.7 | async-start | bytes 9437184 | tf_op jit(solution)/shard_map/all_gather | solution.py:189
  14.4 32.7 %copy-start.62 = (s32[1,4]{1,0:T(1,128)S(1)}, s32[1,4]{1,0:T(1,128)}, u32[]{:S(2)}) copy-start(s32[1,4]{1,0:T(1,128)} %param.31) | copy-start | bytes 52
  14.4 463.9 %all-gather.11.cloned.1.call-start = ((), (), s32[]{:S(2)}) async-start(), calls=%async_computation.8 | async-start | bytes 9437184 | tf_op jit(solution)/shard_map/all_gather | solution.py:189
  17.2 548.5 %reduce-scatter.10.cloned.1.call-start = ((), (), s32[]{:S(2)}) async-start(), calls=%async_computation.10 | async-start | bytes 2359296 | tf_op jit(solution)/shard_map/reduce_scatter | solution.py:278
  46.0 117.4 %copy-start.50 = (f32[1024,1]{0,1:T(1,128)}, f32[1024,1]{0,1:T(1,128)S(1)}, u32[]{:S(2)}) copy-start(f32[1024,1]{0,1:T(1,128)S(1)} %get-tuple-element.201) | copy-start | bytes 12292
  46.0 117.4 %copy-start.60 = (f32[1024,1]{0,1:T(1,128)}, f32[1024,1]{0,1:T(1,128)S(1)}, u32[]{:S(2)}) copy-start(f32[1024,1]{0,1:T(1,128)S(1)} %get-tuple-element.202) | copy-start | bytes 12292
  46.4 117.1 %copy-start.46 = (f32[1024]{0:T(1024)}, f32[1024]{0:T(1024)S(1)}, u32[]{:S(2)}) copy-start(f32[1024]{0:T(1024)S(1)} %broadcast_multiply_fusion.1) | copy-start | bytes 12292
  47.1 116.3 %copy-start.48 = (f32[1024]{0:T(1024)}, f32[1024]{0:T(1024)S(1)}, u32[]{:S(2)}) copy-start(f32[1024]{0:T(1024)S(1)} %fusion.83) | copy-start | bytes 12292
  48.0 150.5 %copy-start.38 = (f32[1024,32]{0,1:T(8,128)}, f32[1024,32]{0,1:T(8,128)S(1)}, u32[]{:S(2)}) copy-start(f32[1024,32]{0,1:T(8,128)S(1)} %get-tuple-element.218) | copy-start | bytes 393220
  48.0 150.5 %copy-start.40 = (f32[1024,32]{0,1:T(8,128)}, f32[1024,32]{0,1:T(8,128)S(1)}, u32[]{:S(2)}) copy-start(f32[1024,32]{0,1:T(8,128)S(1)} %get-tuple-element.219) | copy-start | bytes 393220
  48.9 305.2 %copy-start.14 = (pred[512,1024]{1,0:T(8,128)(4,1)}, pred[512,1024]{1,0:T(8,128)(4,1)S(1)}, u32[]{:S(2)}) copy-start(pred[512,1024]{1,0:T(8,128)(4,1)S(1)} %fusion.57) | copy-start | bytes 1572868
  195.4 56.0 %copy-start.6 = (bf16[1024,16,32]{0,2,1:T(8,128)(2,1)}, bf16[1024,16,32]{0,2,1:T(8,128)(2,1)S(1)}, u32[]{:S(2)}) copy-start(bf16[1024,16,32]{0,2,1:T(8,128)(2,1)S(1)} %slice.370) | copy-start | bytes 3145732
  202.4 49.0 %copy-start.8 = (bf16[1024,16,32]{0,2,1:T(8,128)(2,1)}, bf16[1024,16,32]{0,2,1:T(8,128)(2,1)S(1)}, u32[]{:S(2)}) copy-start(bf16[1024,16,32]{0,2,1:T(8,128)(2,1)S(1)} %get-tuple-element.194) | copy-start | bytes 3145732
  219.6 12.2 %copy-start.44 = (f32[16,512]{1,0:T(8,128)}, f32[16,512]{1,0:T(8,128)S(1)}, u32[]{:S(2)}) copy-start(f32[16,512]{1,0:T(8,128)S(1)} %log_add_fusion.1) | copy-start | bytes 98308
  231.8 15.7 %copy-start.11 = (bf16[1024,16,64]{0,2,1:T(8,128)(2,1)S(1)}, bf16[1024,16,64]{0,2,1:T(8,128)(2,1)}, u32[]{:S(2)}) copy-start(bf16[1024,16,64]{0,2,1:T(8,128)(2,1)} %copy-done.10) | copy-start | bytes 6291460
  265.1 14.8 %copy-start.17 = (bf16[1024,1024]{0,1:T(8,128)(2,1)S(1)}, bf16[1024,1024]{0,1:T(8,128)(2,1)}, u32[]{:S(2)}) copy-start(bf16[1024,1024]{0,1:T(8,128)(2,1)} %copy.72) | copy-start | bytes 6291460
  265.1 14.8 %copy-start.24 = (bf16[512,1024]{0,1:T(8,128)(2,1)S(1)}, bf16[512,1024]{0,1:T(8,128)(2,1)}, u32[]{:S(2)}) copy-start(bf16[512,1024]{0,1:T(8,128)(2,1)} %get-tuple-element.192) | copy-start | bytes 3145732
  279.8 25.1 %copy-start.42 = (f32[16,512]{1,0:T(8,128)}, f32[16,512]{1,0:T(8,128)S(1)}, u32[]{:S(2)}) copy-start(f32[16,512]{1,0:T(8,128)S(1)} %log_add_fusion) | copy-start | bytes 98308
  304.9 28.3 %copy-start.12 = (bf16[1024,16,64]{0,2,1:T(8,128)(2,1)S(1)}, bf16[1024,16,64]{0,2,1:T(8,128)(2,1)}, u32[]{:S(2)}) copy-start(bf16[1024,16,64]{0,2,1:T(8,128)(2,1)} %copy-done.10) | copy-start | bytes 6291460
  333.2 12.6 %copy-start.26 = (bf16[512,1024]{0,1:T(8,128)(2,1)S(1)}, bf16[512,1024]{0,1:T(8,128)(2,1)}, u32[]{:S(2)}) copy-start(bf16[512,1024]{0,1:T(8,128)(2,1)} %copy.68) | copy-start | bytes 3145732
  345.9 8.3 copy-start.18
  345.9 24.5 %slice-start = ((s8[8388608]{0:T(1024)(128)(4,1)}), s8[4194304]{0:T(1024)(128)(4,1)S(1)}, s32[]{:S(2)}) async-start(s8[8388608]{0:T(1024)(128)(4,1)} %bitcast.77), calls=%async_computation.15 | async-start | bytes 8388608
  354.2 16.2 %slice-start.1 = ((s8[8388608]{0:T(1024)(128)(4,1)}), s8[4194304]{0:T(1024)(128)(4,1)S(1)}, s32[]{:S(2)}) async-start(s8[8388608]{0:T(1024)(128)(4,1)} %bitcast.77), calls=%async_computation.16 | async-start | bytes 8388608
  372.7 12.7 %copy-start.41 = (f32[1024,32]{0,1:T(8,128)S(1)}, f32[1024,32]{0,1:T(8,128)}, u32[]{:S(2)}) copy-start(f32[1024,32]{0,1:T(8,128)} %copy-done.40) | copy-start | bytes 393220
  395.2 9.1 copy-start.39
  404.3 201.1 %reduce-scatter.8.cloned.1.call-start = ((), (), s32[]{:S(2)}) async-start(), calls=%async_computation.9 | async-start | bytes 7077888 | tf_op jit(solution)/shard_map/reduce_scatter | solution.py:275
  413.1 17.4 %copy-start.2 = (bf16[1024,1024]{1,0:T(8,128)(2,1)S(1)}, bf16[1024,1024]{1,0:T(8,128)(2,1)}, u32[]{:S(2)}) copy-start(bf16[1024,1024]{1,0:T(8,128)(2,1)} %param.30) | copy-start | bytes 6291460
  413.1 17.4 %copy-start.47 = (f32[1024]{0:T(1024)S(1)}, f32[1024]{0:T(1024)}, u32[]{:S(2)}) copy-start(f32[1024]{0:T(1024)} %copy-done.46) | copy-start | bytes 12292
  413.1 17.4 %copy-start.49 = (f32[1024]{0:T(1024)S(1)}, f32[1024]{0:T(1024)}, u32[]{:S(2)}) copy-start(f32[1024]{0:T(1024)} %copy-done.48) | copy-start | bytes 12292
  413.1 17.4 %copy-start.51 = (f32[1024,1]{0,1:T(1,128)S(1)}, f32[1024,1]{0,1:T(1,128)}, u32[]{:S(2)}) copy-start(f32[1024,1]{0,1:T(1,128)} %copy-done.50) | copy-start | bytes 12292
  413.1 17.4 %copy-start.61 = (f32[1024,1]{0,1:T(1,128)S(1)}, f32[1024,1]{0,1:T(1,128)}, u32[]{:S(2)}) copy-start(f32[1024,1]{0,1:T(1,128)} %copy-done.60) | copy-start | bytes 12292
  443.2 314.0 %reduce-scatter.14.cloned.1.call-start = ((), (), s32[]{:S(2)}) async-start(), calls=%async_computation.12 | async-start | bytes 9437184 | tf_op jit(solution)/shard_map/reduce_scatter | solution.py:284
  444.2 15.6 %copy-start.21 = (bf16[1024,1024]{1,0:T(8,128)(2,1)S(1)}, bf16[1024,1024]{1,0:T(8,128)(2,1)}, u32[]{:S(2)}) copy-start(bf16[1024,1024]{1,0:T(8,128)(2,1)} %param.32) | copy-start | bytes 6291460
  478.3 431.0 %reduce-scatter.12.cloned.1.call-start = ((), (), s32[]{:S(2)}) async-start(), calls=%async_computation.11 | async-start | bytes 9437184 | tf_op jit(solution)/shard_map/reduce_scatter | solution.py:281
  519.5 453.9 %reduce-scatter.16.cloned.1.call-start = ((), (), s32[]{:S(2)}) async-start(), calls=%async_computation.13 | async-start | bytes 294912
  538.6 15.1 %copy-start.53 = (f32[1024]{0:T(1024)S(1)}, f32[1024]{0:T(1024)}, u32[]{:S(2)}) copy-start(f32[1024]{0:T(1024)} %copy-done.52) | copy-start | bytes 12292
  559.1 350.3 %copy-start.58 = (f32[1024,1]{0,1:T(1,128)S(1)}, f32[1024,1]{0,1:T(1,128)}, u32[]{:S(2)}) copy-start(f32[1024,1]{0,1:T(1,128)} %get-tuple-element.199) | copy-start | bytes 12292
  559.1 350.3 %copy-start.59 = (f32[1024,1]{0,1:T(1,128)S(1)}, f32[1024,1]{0,1:T(1,128)}, u32[]{:S(2)}) copy-start(f32[1024,1]{0,1:T(1,128)} %get-tuple-element.200) | copy-start | bytes 12292
  559.1 484.8 %all-reduce.5.cloned.1.call-start = ((), (), s32[]{:S(2)}) async-start(), calls=%async_computation.14 | async-start | bytes 6291456 | tf_op jit(solution)/shard_map/psum | solution.py:290
  1055.7 28.1 %copy-start.55 = (f32[128,11]{0,1:T(8,128)S(1)}, f32[128,11]{0,1:T(8,128)}, u32[]{:S(2)}) copy-start(f32[128,11]{0,1:T(8,128)} %param.45) | copy-start | bytes 16900
  1055.7 28.1 %copy-start.56 = (f32[128,11]{0,1:T(8,128)S(1)}, f32[128,11]{0,1:T(8,128)}, u32[]{:S(2)}) copy-start(f32[128,11]{0,1:T(8,128)} %param.47) | copy-start | bytes 16900
  1055.8 28.1 %copy-start.57 = (f32[128,11]{0,1:T(8,128)S(1)}, f32[128,11]{0,1:T(8,128)}, u32[]{:S(2)}) copy-start(f32[128,11]{0,1:T(8,128)} %param.46) | copy-start | bytes 16900
  1055.8 28.7 %copy-start.32 = (f32[128,1024]{1,0:T(8,128)S(1)}, f32[128,1024]{1,0:T(8,128)}, u32[]{:S(2)}) copy-start(f32[128,1024]{1,0:T(8,128)} %param.36) | copy-start | bytes 1572868
  1055.8 31.4 %copy-start.30 = (bf16[128,3072]{1,0:T(8,128)(2,1)S(1)}, bf16[128,3072]{1,0:T(8,128)(2,1)}, u32[]{:S(2)}) copy-start(bf16[128,3072]{1,0:T(8,128)(2,1)} %get-tuple-element.159) | copy-start | bytes 2359300
  1060.9 26.3 %copy-start.25 = (f32[128,3072]{1,0:T(8,128)S(1)}, f32[128,3072]{1,0:T(8,128)}, u32[]{:S(2)}) copy-start(f32[128,3072]{1,0:T(8,128)} %param.33) | copy-start | bytes 4718596
  (27 other events, 96.6 us)
Sparse Core Ops, SparseCore 0:
  10.7 52.3 all-gather.6
  65.9 97.5 all-gather.4
  166.1 123.1 all-gather.8
  291.8 123.1 all-gather.10
  418.9 65.9 reduce-scatter.9
  488.4 116.9 reduce-scatter.7
  609.0 148.1 reduce-scatter.13
  761.3 147.9 reduce-scatter.11
  913.2 60.1 reduce-scatter.15
  975.8 68.0 all-reduce.4
where the time goes:
time: 1110 us
  waiting for transfers between devices  561 us (51%)
  matrix products  293 us (26%)
  other arithmetic  136 us (12%)
  blocking collectives  55.9 us (5%)
  local copies, waits for them, and re-layouts  42.5 us (4%)
  between operations  20.4 us (2%)
    reduce_scatter x1, waiting for transfers between devices, body(): lax.psum_scatter(local_grads[3].astype(jnp.bfloat16), 'shard', scatter_di...  152 us
    reduce_scatter x1, waiting for transfers between devices, body(): lax.psum_scatter(local_grads[4].astype(jnp.bfloat16), 'shard', scatter_di...  152 us
    all_gather x4, waiting for transfers between devices, body(): lax.all_gather(shortened(shards), 'shard', axis=0, tiled=True)  108 us
    psum x1, waiting for transfers between devices, body(): lax.psum(owned[1].astype(jnp.bfloat16), 'rep').astype(jnp.float32)  63.4 us
    unnamed x11, waiting for transfers between devices  45.4 us
    convert_element_type x2, other arithmetic, attend_backward(): grad_scores = (probs * (grad_probs - inner)).astype(jnp.bfloat16)  40.6 us
    reduce_scatter x1, waiting for transfers between devices, body(): lax.psum_scatter(local_grads[1].astype(jnp.bfloat16), 'shard', scatter_di...  39.6 us
    dot_general x2, matrix products, attend_backward(): jnp.einsum('qhd,khd->hqk', rows_grad, seq_values[:key_stop], preferred_el...  37.2 us
  transfers between devices with their start and end apart: 10, of which 7 were waited for; matrix products, arithmetic and copies ran while one was open for 38% of the time, Pallas kernels for 0%

commit v1 on v0

v1 whole, which is shorter than its diff:
```python
import math

import jax
import jax.numpy as jnp
from jax import lax
from jax.experimental import pallas as pl
from jax.experimental.pallas import tpu as pltpu
from jax.sharding import PartitionSpec as P

D = 1024
HEADS = 16
HEAD_DIM = 64
ROTARY = 32
FF = 4096
LEN = 1024
STEP = 10
VROWS = 11
VPAD = 16
UNITS = 12
QB = 256

clip_limit = 1.0
matrix_rate = 0.05
vector_rate = 0.8
decay_rate = 0.1

BF = jnp.bfloat16
F32 = jnp.float32
MIB = 1 << 20


def dot(a, b, ca, cb):
    return lax.dot_general(a, b, (((ca,), (cb,)), ((), ())), preferred_element_type=F32)


class Place:
    def __init__(self, nz):
        self.nz = nz
        self.r = lax.axis_index("rep")
        self.s = lax.axis_index("shard")
        self.z, self.x = self.s // 2, self.s % 2
        self.c = self.r % 2
        self.y = (self.r // 2) % 2
        self.p = 2 * self.c + self.y

    def dev(self, r, s):
        return {"rep": r, "shard": s}

    def zpeer(self, k):
        return self.dev(self.r, ((self.z + k) % self.nz) * 2 + self.x)

    @property
    def xpeer(self):
        return self.dev(self.r, self.z * 2 + 1 - self.x)

    @property
    def ypeer(self):
        return self.dev(self.r + 2 - 4 * self.y, self.s)

    @property
    def cpeer(self):
        return self.dev(self.r + 1 - 2 * self.c, self.s)

    @property
    def diag(self):
        return self.dev(self.r + 2 - 4 * self.y + 1 - 2 * self.c, self.s)

    def swap(self, first):
        on_x = self.c == (0 if first else 1)
        return self.dev(
            jnp.where(on_x, self.r, self.r + 2 - 4 * self.y),
            jnp.where(on_x, self.z * 2 + 1 - self.x, self.s),
        )


def greet(peers):
    barrier = pltpu.get_barrier_semaphore()
    for peer in peers:
        pl.semaphore_signal(barrier, inc=1, device_id=peer, device_id_type=pl.DeviceIdType.MESH)
    pl.semaphore_wait(barrier, len(peers))


def remote(src, dst, send, recv, peer):
    return pltpu.make_async_remote_copy(
        src_ref=src,
        dst_ref=dst,
        send_sem=send,
        recv_sem=recv,
        device_id=peer,
        device_id_type=pl.DeviceIdType.MESH,
    )


class Gather:
    def __init__(self, at, own, full, u0, n, send, recv, base):
        self.at, self.own, self.full = at, own, full
        self.us = pl.ds(u0, n)
        self.send, self.recv, self.base = send, recv, base

    @staticmethod
    def sems(nz):
        return (nz - 1) + nz + 2 * nz + 2 * nz

    def block(self, k, other):
        at = self.at
        zk = (at.z + at.nz - k) % at.nz
        return zk * 2 + (1 - at.x if other else at.x)

    def copy(self, sem, src, dst, peer):
        i = self.base + sem
        return remote(src, dst, self.send.at[i], self.recv.at[i], peer)

    def rows(self, y):
        return pl.ds(self.at.c * 64 + y * 32, 32)

    def mine(self, k):
        return self.own.at[self.us, self.rows(self.at.y)] if k == 0 else self.full.at[
            self.us, self.block(k, False), self.rows(self.at.y)
        ]

    def send_z(self, k):
        dst = self.full.at[self.us, self.at.s, self.rows(self.at.y)]
        return self.copy(k - 1, self.mine(0), dst, self.at.zpeer(k))

    def recv_z(self, k):
        dst = self.full.at[self.us, self.block(k, False), self.rows(self.at.y)]
        return self.copy(k - 1, self.mine(0), dst, self.at.zpeer(k))

    def place_a(self, k):
        at = self.at
        zk = (at.z + at.nz - k) % at.nz
        block = zk * 2 + jnp.where(at.c == 0, 1 - at.x, at.x)
        return self.full.at[self.us, block, self.rows(jnp.where(at.c == 0, at.y, 1 - at.y))]

    def send_a(self, k):
        dst = self.full.at[self.us, self.block(k, False), self.rows(self.at.y)]
        return self.copy(self.at.nz - 1 + k, self.mine(k), dst, self.at.swap(True))

    def recv_a(self, k):
        return self.copy(self.at.nz - 1 + k, self.mine(k), self.place_a(k), self.at.swap(True))

    def send_b(self, k, j):
        i = 2 * self.at.nz - 1 + 2 * k + j
        if j == 0:
            dst = self.full.at[self.us, self.block(k, False), self.rows(self.at.y)]
            return self.copy(i, self.mine(k), dst, self.at.swap(False))
        return self.copy(i, self.place_a(k), self.place_a(k), self.at.swap(False))

    def own_b(self):
        src = self.own.at[self.us, self.rows(1 - self.at.y)]
        return self.copy(2 * self.at.nz, src, self.place_a(0), self.at.swap(False))

    def recv_b(self, k, j):
        at = self.at
        i = 2 * at.nz - 1 + 2 * k + j
        zk = (at.z + at.nz - k) % at.nz
        if j == 0:
            block = zk * 2 + jnp.where(at.c == 0, at.x, 1 - at.x)
            dst = self.full.at[self.us, block, self.rows(jnp.where(at.c == 0, 1 - at.y, at.y))]
        else:
            dst = self.full.at[self.us, zk * 2 + 1 - at.x, self.rows(1 - at.y)]
        return self.copy(i, dst, dst, at.swap(False))

    def send_c(self, k, other):
        i = 4 * self.at.nz - 1 + 2 * k + other
        ref = self.full.at[self.us, self.block(k, other), pl.ds(self.at.c * 64, 64)]
        return self.copy(i, ref, ref, self.at.cpeer)

    def recv_c(self, k, other):
        i = 4 * self.at.nz - 1 + 2 * k + other
        ref = self.full.at[self.us, self.block(k, other), pl.ds((1 - self.at.c) * 64, 64)]
        return self.copy(i, ref, ref, self.at.cpeer)

    def only(self, core, what):
        pl.when(self.at.c == core)(what)

    def stage0(self):
        for k in range(1, self.at.nz):
            self.send_z(k).start()
        self.only(0, lambda: self.send_a(0).start())
        self.only(1, lambda: self.send_b(0, 0).start())

    def stage1(self):
        for k in range(1, self.at.nz):
            self.recv_z(k).wait_recv()
            self.send_a(k).start()
            self.send_b(k, 0).start()

    def stage2(self):
        for k in range(self.at.nz):
            if k == 0:
                self.only(0, lambda: self.recv_a(0).wait_recv())
                self.only(0, lambda: self.send_b(0, 1).start())
                self.only(1, lambda: self.own_b().start())
            else:
                self.recv_a(k).wait_recv()
                self.send_b(k, 1).start()

    def stage3(self):
        for k in range(self.at.nz):
            if k == 0:
                self.only(1, lambda: self.recv_b(0, 0).wait_recv())
            else:
                self.recv_b(k, 0).wait_recv()
                self.send_c(k, 0).start()
            self.recv_b(k, 1).wait_recv()
            self.send_c(k, 1).start()

    def stage4(self):
        for k in range(self.at.nz):
            if k:
                self.recv_c(k, 0).wait_recv()
            self.recv_c(k, 1).wait_recv()
        for k in range(1, self.at.nz):
            self.send_z(k).wait_send()
        for k in range(self.at.nz):
            if k:
                self.send_a(k).wait_send()
                self.send_b(k, 0).wait_send()
                self.send_c(k, 0).wait_send()
            else:
                self.only(0, lambda: self.send_a(0).wait_send())
                self.only(1, lambda: self.send_b(0, 0).wait_send())
            self.send_b(k, 1).wait_send()
            self.send_c(k, 1).wait_send()


def rotate_rows(u, cosine, sine):
    top = u[:16] * cosine - u[16:32] * sine
    low = u[16:32] * cosine + u[:16] * sine
    return jnp.concatenate([top, low, u[32:]], axis=0)


def head_attention(rows, outs, bias, qt, kt, vt, gt, act, dqt, dkt, dvt):
    for number in range(LEN // QB):
        q0 = number * QB
        k0 = max(0, number - 2) * QB
        span = q0 + QB - k0
        q = qt[rows, q0 : q0 + QB]
        g = gt[rows, q0 : q0 + QB]
        k = kt[rows, k0 : k0 + span]
        v = vt[rows, k0 : k0 + span]
        s = dot(k, q, 0, 0) + bias[number, :span]
        e = jnp.exp(s - jnp.max(s, axis=0, keepdims=True))
        p = e * (1.0 / jnp.sum(e, axis=0, keepdims=True))
        pb = p.astype(BF)
        o = dot(v, pb, 1, 0)
        dp = dot(v, g, 0, 0)
        inner = jnp.sum(o * g.astype(F32), axis=0, keepdims=True)
        ds = (p * (dp - inner)).astype(BF)
        act[0, outs, q0 : q0 + QB] = o.astype(BF)
        dqt[:, q0 : q0 + QB] = dot(k, ds, 1, 0)
        dk = dot(q, ds, 1, 1)
        dv = dot(g, pb, 1, 1)
        old = span - QB
        if old:
            dkt[:, k0 : k0 + old] += dk[:, :old]
            dvt[:, k0 : k0 + old] += dv[:, :old]
        dkt[:, q0 : q0 + QB] = dk[:, old:]
        dvt[:, q0 : q0 + QB] = dv[:, old:]


class GatherGroup(Gather):
    def __init__(self, at, own, full, u0, n, send, recv, row):
        super().__init__(at, own, full, u0, n, send, recv, 0)
        self.row = row

    def copy(self, sem, src, dst, peer):
        return remote(src, dst, self.send.at[self.row, sem], self.recv.at[self.row, sem], peer)


def run_stage(gather, stage):
    getattr(gather, f"stage{stage}")()


def front_kernel(
    nz,
    lengths, tokens, dy, wqkv, wd, vec, wexpand, wshrink,
    full, table, ht, act,
    own, expand_f, shrink_f, weights, bias, cosine, sine, qt, kt, vt, gt, dqf, dkf, dvf,
    send_a, recv_a, send_f, recv_f, vsend, vrecv, lsem,
):
    at = Place(nz)
    shards = 2 * nz
    others = [at.dev(at.r, (at.s + k) % shards) for k in range(1, shards)]
    load_expand = pltpu.make_async_copy(wexpand, expand_f, lsem.at[0])
    load_shrink = pltpu.make_async_copy(wshrink, shrink_f, lsem.at[1])
    load_expand.start()
    load_shrink.start()
    own[0] = wd[...].astype(BF)
    for i in range(3):
        own[1 + i] = wqkv[:, i * D : i * D + D].astype(BF)
    greet(others + [at.ypeer, at.cpeer])

    def lanes(i):
        return pl.ds(pl.multiple_of(i * 128, 128), 128)

    vcopies = [
        remote(vec, table.at[:, lanes(at.s)], vsend.at[k], vrecv.at[k], peer)
        for k, peer in enumerate(others)
    ]
    for copy in vcopies:
        copy.start()
    table[:, lanes(at.s)] = vec[...]
    local_a = pltpu.make_async_copy(own.at[0:4], full.at[0:4, at.s], lsem.at[2])
    local_a.start()
    first = [GatherGroup(at, own, full, u, 1, send_a, recv_a, u) for u in range(4)]
    local_f = pltpu.make_async_copy(own.at[4:UNITS], full.at[4:UNITS, at.s], lsem.at[3])

    def cast_rest():
        load_expand.wait()
        load_shrink.wait()
        width = FF // shards
        for j in range(FF // D):
            own[4 + 2 * j] = shrink_f[j * 128 : j * 128 + 128].astype(BF)
            for b in range(shards):
                own[5 + 2 * j, :, b * 128 : b * 128 + 128] = expand_f[
                    :, b * width + j * 128 : b * width + j * 128 + 128
                ].astype(BF)
        local_f.start()

    def tables():
        place = lax.broadcasted_iota(jnp.int32, (1, LEN), 1)
        start = jnp.zeros((1, LEN), jnp.int32)
        end = 0
        for d in range(lengths.shape[1]):
            end = end + lengths[0, d]
            start = start + jnp.where(place >= end, lengths[0, d], 0)
        m = lax.broadcasted_iota(jnp.int32, (ROTARY // 2, LEN), 0).astype(F32)
        frequency = jnp.exp(m * (-2.0 * math.log(10000.0) / ROTARY))
        angle = (place - start).astype(F32) * frequency
        cosine[...] = jnp.cos(angle)
        sine[...] = jnp.sin(angle)
        for number in range(LEN // QB):
            q0 = number * QB
            k0 = max(0, number - 2) * QB
            span = q0 + QB - k0
            j = k0 + lax.broadcasted_iota(jnp.int32, (span, QB), 0)
            i = q0 + lax.broadcasted_iota(jnp.int32, (span, QB), 1)
            allowed = (j >= start[:, q0 : q0 + QB]) & (j <= i)
            bias[number, :span] = jnp.where(allowed, 0.0, -1e30)

    def wait_vec():
        for k, copy in enumerate(vcopies):
            came = (at.s + shards - (k + 1)) % shards
            remote(vec, table.at[:, lanes(came)], vsend.at[k], vrecv.at[k], others[k]).wait_recv()
            copy.wait_send()

    def norm_rows(i):
        rows = pl.ds(pl.multiple_of(i * 256, 256), 256)
        x = tokens[rows].astype(F32)
        centered = x - jnp.mean(x, axis=1, keepdims=True)
        scaled = centered * lax.rsqrt(jnp.mean(centered * centered, axis=1, keepdims=True) + 1e-05)
        h = scaled * table[0:1].astype(F32) + table[1:2].astype(F32)
        ht[:, rows] = h.astype(BF).T

    side = {0: cast_rest, 1: tables, 2: wait_vec}
    for i in range(4):
        side[3 + i] = lambda i=i: norm_rows(i)

    def later_step(t):
        for stage in range(5):
            g = t - stage

            def go(g=g, stage=stage):
                run_stage(GatherGroup(at, own, full, 4 + 2 * g, 2, send_f, recv_f, g), stage)

            if isinstance(g, int):
                if 0 <= g < 4:
                    go()
            else:
                pl.when((g >= 0) & (g < 4))(go)

    def load_weights(u):
        return pltpu.make_async_copy(full.at[u], weights.at[u], lsem.at[4 + u])

    for step in range(8):
        for stage in range(5):
            if 0 <= step - stage < 4:
                run_stage(first[step - stage], stage)
                if stage == 4:
                    if step == 4:
                        local_a.wait()
                    load_weights(step - stage).start()
        if step in side:
            side[step]()
        if step == 5:
            later_step(0)
        if step == 7:
            later_step(1)
    for u in range(4):
        load_weights(u).wait()

    def prepare(quad):
        cols = pl.ds(pl.multiple_of(quad * 256, 256), 256)
        for part, dst in enumerate((qt, kt, vt)):
            w = weights[1 + part, :, :, cols].reshape(D, 256)
            u = dot(w, ht[...], 0, 0)
            ones = jnp.ones((1, 128), BF)
            b = dot(table[2 + part : 3 + part, cols], ones, 0, 0)[:, :1]
            u = u + b
            if part == 2:
                dst[...] = u.astype(BF)
                continue
            for head in range(4):
                turned = rotate_rows(u[head * 64 : head * 64 + 64], cosine[...], sine[...])
                if part == 0:
                    turned = turned * (1.0 / math.sqrt(HEAD_DIM))
                dst[head * 64 : head * 64 + 64] = turned.astype(BF)
        for half in range(2):
            w = weights[0, 2 * quad + half]
            gt[half * 128 : half * 128 + 128] = dot(w, dy[...], 1, 1).astype(BF)

    def one_head(number, carry):
        quad, head = number // 4, number % 4
        pl.when(head == 0)(lambda: prepare(quad))
        rows = pl.ds(pl.multiple_of(head * 64, 64), 64)
        outs = pl.ds(pl.multiple_of(number * 64, 64), 64)
        head_attention(rows, outs, bias, qt, kt, vt, gt, act, dqf, dkf, dvf)
        back = rotate_rows(dqf[...], cosine[...], -sine[...]) * (1.0 / math.sqrt(HEAD_DIM))
        act[1, outs] = back.astype(BF)
        act[2, outs] = rotate_rows(dkf[...], cosine[...], -sine[...]).astype(BF)
        act[3, outs] = dvf[...].astype(BF)
        t = 2 + number // 2
        pl.when((number % 2 == 1) & (t < 8))(lambda: later_step(t))
        return carry

    lax.fori_loop(0, HEADS, one_head, 0)
    local_f.wait()


def front(lengths, tokens, dy, wqkv, wd, vec, wexpand, wshrink, nz):
    shards = 2 * nz
    count = Gather.sems(nz)
    anywhere = pl.BlockSpec(memory_space=pl.ANY)
    inside = pl.BlockSpec(memory_space=pltpu.VMEM)

    def kernel(*refs):
        front_kernel(nz, *refs)

    return pl.pallas_call(
        kernel,
        out_shape=(
            jax.ShapeDtypeStruct((UNITS, shards, 128, D), BF),
            jax.ShapeDtypeStruct((VPAD, D), BF),
            jax.ShapeDtypeStruct((D, LEN), BF),
            jax.ShapeDtypeStruct((4, D, LEN), BF),
        ),
        in_specs=[
            pl.BlockSpec(memory_space=pltpu.SMEM),
            inside,
            inside,
            inside,
            inside,
            inside,
            anywhere,
            anywhere,
        ],
        out_specs=(anywhere, inside, inside, inside),
        scratch_shapes=[
            pltpu.VMEM((UNITS, 128, D), BF),
            pltpu.VMEM(wexpand.shape, F32),
            pltpu.VMEM(wshrink.shape, F32),
            pltpu.VMEM((4, shards, 128, D), BF),
            pltpu.VMEM((LEN // QB, 3 * QB, QB), F32),
            pltpu.VMEM((ROTARY // 2, LEN), F32),
            pltpu.VMEM((ROTARY // 2, LEN), F32),
            pltpu.VMEM((256, LEN), BF),
            pltpu.VMEM((256, LEN), BF),
            pltpu.VMEM((256, LEN), BF),
            pltpu.VMEM((256, LEN), BF),
            pltpu.VMEM((64, LEN), F32),
            pltpu.VMEM((64, LEN), F32),
            pltpu.VMEM((64, LEN), F32),
            pltpu.SemaphoreType.DMA((4, count)),
            pltpu.SemaphoreType.DMA((4, count)),
            pltpu.SemaphoreType.DMA((4, count)),
            pltpu.SemaphoreType.DMA((4, count)),
            pltpu.SemaphoreType.DMA((shards - 1,)),
            pltpu.SemaphoreType.DMA((shards - 1,)),
            pltpu.SemaphoreType.DMA((8,)),
        ],
        compiler_params=pltpu.CompilerParams(
            collective_id=0, has_side_effects=True, vmem_limit_bytes=58 * MIB
        ),
        name="front",
    )(lengths, tokens, dy, wqkv, wd, vec, wexpand, wshrink)


RC = 4


class Reduce:
    def __init__(self, at, grads, rc, rb, ra, rz, out, send, recv):
        self.at = at
        self.grads, self.rc, self.rb, self.ra, self.rz, self.out = grads, rc, rb, ra, rz, out
        self.send, self.recv = send, recv

    @staticmethod
    def sems(nz):
        return 3 + (nz - 1) + 3

    def copy(self, u, i, src, dst, peer):
        return remote(src, dst, self.send.at[u, i], self.recv.at[u, i], peer)

    def c(self, u):
        at = self.at
        return self.copy(u, 0, self.grads.at[u % 2, :, :, 1 - at.c], self.rc.at[u % RC], at.cpeer)

    def b(self, u, core):
        at = self.at
        rc = self.rc.at[u % RC]
        src = rc.at[:, :, 1 - at.y] if core == 0 else rc.at[:, 1 - at.x]
        return self.copy(u, 1, src, self.rb.at[u], at.swap(False))

    def turn(self):
        return jnp.where(self.at.c == 0, self.at.x, self.at.y)

    def a(self, u):
        src = self.rb.at[u, :, 1 - self.turn()]
        return self.copy(u, 2, src, self.ra.at[u], self.at.swap(True))

    def z(self, u, k):
        at = self.at
        src = self.ra.at[u, (at.z + k) % at.nz]
        return self.copy(u, 2 + k, src, self.rz.at[u, k - 1], at.zpeer(k))

    def f(self, u, k):
        at = self.at
        ref = self.out.at[u, at.p]
        return self.copy(u, 2 + at.nz + k, ref, ref, (at.ypeer, at.cpeer, at.diag)[k])

    def f_in(self, u, k):
        at = self.at
        c, y = (at.c if k == 0 else 1 - at.c), (at.y if k == 1 else 1 - at.y)
        ref = self.out.at[u, 2 * c + y]
        return self.copy(u, 2 + at.nz + k, ref, ref, (at.ypeer, at.cpeer, at.diag)[k])

    def phase0(self, u):
        self.c(u).start()

    def phase1(self, u):
        at = self.at
        self.c(u).wait_recv()
        add_into(self.rc.at[u % RC], self.grads.at[u % 2, :, :, at.c])
        for core in (0, 1):
            pl.when(at.c == core)(lambda core=core: self.b(u, core).start())

    def phase2(self, u):
        at = self.at
        rc = self.rc.at[u % RC]
        self.b(u, 0).wait_recv()
        pl.when(at.c == 0)(lambda: add_into(self.rb.at[u], rc.at[:, :, at.y]))
        pl.when(at.c == 1)(lambda: add_into(self.rb.at[u], rc.at[:, at.x]))
        self.a(u).start()
        self.b(u, 0).wait_send()
        self.c(u).wait_send()

    def phase3(self, u):
        self.a(u).wait_recv()
        add_into(self.ra.at[u], self.rb.at[u, :, self.turn()])
        for k in range(1, self.at.nz):
            self.z(u, k).start()

    def phase4(self, u):
        at = self.at
        total = self.ra[u, at.z].astype(F32)
        for k in range(1, at.nz):
            self.z(u, k).wait_recv()
            total += self.rz[u, k - 1].astype(F32)
        self.out[u, at.p] = total.astype(BF)
        for k in range(3):
            self.f(u, k).start()

    def phase5(self, u):
        for k in range(3):
            self.f_in(u, k).wait_recv()
            self.f(u, k).wait_send()
        self.a(u).wait_send()
        for k in range(1, self.at.nz):
            self.z(u, k).wait_send()


PHASES = 6


def add_into(dst, src):
    dst[...] = (dst[...].astype(F32) + src[...].astype(F32)).astype(BF)


class VecSum:
    def __init__(self, shards, reps, gvec, v1, v2, sq, send, recv):
        self.shards, self.reps = shards, reps
        self.r, self.s = lax.axis_index("rep"), lax.axis_index("shard")
        self.row = [{"rep": self.r, "shard": (self.s + k) % shards} for k in range(1, shards)]
        self.col = [{"rep": (self.r + k) % reps, "shard": self.s} for k in range(1, reps)]
        self.gvec, self.v1, self.v2, self.sq = gvec, v1, v2, sq
        self.send, self.recv = send, recv

    @staticmethod
    def sems(shards, reps):
        return 2 * (shards - 1) + reps - 1

    def lanes(self, i):
        return pl.ds(pl.multiple_of(i * 128, 128), 128)

    def copy(self, i, src, dst, peer):
        return remote(src, dst, self.send.at[i], self.recv.at[i], peer)

    def over_shards(self, k):
        src = self.gvec.at[:, self.lanes((self.s + k) % self.shards)]
        return self.copy(k - 1, src, self.v1.at[self.s], self.row[k - 1])

    def over_reps(self, k):
        ref = self.v2.at[self.r]
        return self.copy(self.shards + k - 2, ref, ref, self.col[k - 1])

    def squares(self, k):
        ref = self.sq.at[self.s]
        return self.copy(self.shards + self.reps + k - 3, ref, ref, self.row[k - 1])

    def total(self, ref, count):
        every = ref[0]
        for i in range(1, count):
            every += ref[i]
        return every

    def stage0(self):
        for k in range(1, self.shards):
            self.over_shards(k).start()
        self.v1[self.s] = self.gvec[:, self.lanes(self.s)]

    def stage1(self):
        for k in range(1, self.shards):
            dst = self.v1.at[(self.s + self.shards - k) % self.shards]
            self.copy(k - 1, dst, dst, self.row[k - 1]).wait_recv()
            self.over_shards(k).wait_send()
        self.v2[self.r] = self.total(self.v1, self.shards)
        for k in range(1, self.reps):
            self.over_reps(k).start()

    def stage2(self):
        for k in range(1, self.reps):
            dst = self.v2.at[(self.r + self.reps - k) % self.reps]
            self.copy(self.shards + k - 2, dst, dst, self.col[k - 1]).wait_recv()
            self.over_reps(k).wait_send()
        return self.total(self.v2, self.reps)

    def norm(self, wide, table):
        part = table[:8] * table[:8] + table[8:] * table[8:]
        for i in range(D // 128):
            part += wide[:, i * 128 : i * 128 + 128]
        self.sq[self.s] = part
        for k in range(1, self.shards):
            self.squares(k).start()
        for k in range(1, self.shards):
            i = self.shards + self.reps + k - 3
            dst = self.sq.at[(self.s + self.shards - k) % self.shards]
            self.copy(i, dst, dst, self.row[k - 1]).wait_recv()
            self.squares(k).wait_send()
        return jnp.sqrt(jnp.sum(self.total(self.sq, self.shards), keepdims=True))


def fold_squares(block):
    g = block.astype(F32)
    return jnp.sum((g * g).reshape(-1, 8, D), axis=0)


def cols(n):
    return pl.ds(pl.multiple_of(n * 256, 256), 256)


def tiles(run):
    def one(n, carry):
        run(n)
        return carry

    lax.fori_loop(0, D // 256, one, 0)


def back_kernel(
    nz, reps,
    tokens, dy, ht, table, act, full,
    out, grad_in, owned, gtable, norm,
    wb, grads, rc, rb, ra, rz, gelu, dact, acc, b1, gb1, gv, wide, v1, v2, sq,
    send, recv, vsend, vrecv, wsem,
):
    at = Place(nz)
    shards = 2 * nz
    fused = reps == 4
    width = FF // shards
    load_first = lambda q, src: pltpu.make_async_copy(src, wb.at[q % 2, 0], wsem.at[q % 2, 0])
    load_second = lambda q, src: pltpu.make_async_copy(src, wb.at[q % 2, 1], wsem.at[q % 2, 1])

    load_first(0, act.at[0]).start()
    load_second(0, full.at[0]).start()
    red = Reduce(at, grads, rc, rb, ra, rz, owned, send, recv)
    vecs = VecSum(shards, reps, gv, v1, v2, sq, vsend, vrecv)
    gv[...] = jnp.zeros((VPAD, D), F32)
    wide[...] = jnp.zeros((8, D), F32)
    for j in range(FF // D):
        for s in range(shards):
            f = s * width + j * 128
            b1[j : j + 1, s * 128 : s * 128 + 128] = table[
                6 + f // D : 7 + f // D, f % D : f % D + 128
            ].astype(F32)
    greet(vecs.row + [at.ypeer, at.cpeer, at.diag])

    def write(u, n, value):
        grads[u % 2, :, :, :, :, :, cols(n)] = value.astype(BF).reshape(nz, 2, 2, 2, 32, 256)

    def activate(slot, j):
        def tile(n):
            a = dot(ht[...], wb[slot, 1, :, cols(n)], 0, 0) + b1[pl.ds(j, 1), cols(n)]
            square = a * a
            t = jnp.tanh(math.sqrt(2.0 / math.pi) * a * (1.0 + 0.044715 * square))
            half = 0.5 * (1.0 + t)
            gelu[:, cols(n)] = (a * half).astype(BF)
            slope = half + 0.5 * a * (1.0 - t * t) * (
                math.sqrt(2.0 / math.pi) * (1.0 + 3 * 0.044715 * square)
            )
            da = (dot(dy[...], wb[slot, 0, cols(n), :], 1, 1) * slope).astype(BF)
            dact[:, cols(n)] = da
            gb1[pl.ds(j, 1), cols(n)] = jnp.sum(da.astype(F32), axis=0, keepdims=True)

        tiles(tile)

    def finish():
        gain = table[0:1].astype(F32)
        shift = table[5:6].astype(F32) + table[10:11].astype(F32)

        def rows_of(i, carry):
            rows = pl.ds(pl.multiple_of(i * 128, 128), 128)
            x = tokens[rows].astype(F32)
            out[rows] = (x + acc[rows] + shift).astype(BF)
            centered = x - jnp.mean(x, axis=1, keepdims=True)
            rstd = lax.rsqrt(jnp.mean(centered * centered, axis=1, keepdims=True) + 1e-05)
            n = centered * rstd
            dh = grad_in[rows]
            back = dy[rows].astype(F32)
            e = dh * gain
            grad_in[rows] = back + rstd * (
                e
                - jnp.mean(e, axis=1, keepdims=True)
                - n * jnp.mean(e * n, axis=1, keepdims=True)
            )
            gv[0:1] += jnp.sum(dh * n, axis=0, keepdims=True)
            gv[1:2] += jnp.sum(dh, axis=0, keepdims=True)
            gv[5:6] += jnp.sum(back, axis=0, keepdims=True)
            return carry

        lax.fori_loop(0, LEN // 128, rows_of, 0)
        gv[10:11] = gv[5:6]
        for j in range(FF // D):
            for s in range(shards):
                f = s * width + j * 128
                gv[6 + f // D : 7 + f // D, f % D : f % D + 128] = gb1[
                    j : j + 1, s * 128 : s * 128 + 128
                ]

    def tick(t, carry):
        for number in range(1, PHASES):
            u = t - number

            def phase(u=u, number=number):
                getattr(red, f"phase{number}")(u)
                if number == 5 and fused:
                    wide[...] += fold_squares(owned[u])

            pl.when((u >= 0) & (u < UNITS))(phase)

        q = jnp.where(t < 4, t, 4 + (t - 4) // 2)
        slot = q % 2
        j = q - 4

        @pl.when((t < UNITS) & ((t < 4) | (t % 2 == 0)))
        def _():
            load_first(q, full.at[0]).wait()
            load_second(q, full.at[0]).wait()

            @pl.when(q + 1 < 4)
            def _():
                load_first(q + 1, act.at[q + 1]).start()
                load_second(q + 1, full.at[q + 1]).start()

            @pl.when((q + 1 >= 4) & (q + 1 < 8))
            def _():
                load_first(q + 1, full.at[2 * (q + 1) - 4]).start()
                load_second(q + 1, full.at[2 * (q + 1) - 3]).start()

        dense, qkv = t == 0, (t >= 1) & (t < 4)
        mlp = (t >= 4) & (t < UNITS)
        shrink, expand = mlp & (t % 2 == 0), mlp & (t % 2 == 1)

        pl.when(shrink)(lambda: activate(slot, j))
        pl.when(dense)(
            lambda: tiles(lambda n: write(t, n, dot(wb[slot, 0], dy[:, cols(n)], 1, 0)))
        )
        pl.when(qkv)(
            lambda: tiles(lambda n: write(t, n, dot(ht[...], wb[slot, 0, cols(n), :], 1, 1)))
        )
        pl.when(shrink)(
            lambda: tiles(lambda n: write(t, n, dot(gelu[...], dy[:, cols(n)], 0, 0)))
        )
        pl.when(expand)(
            lambda: tiles(lambda n: write(t, n, dot(ht[...], dact[:, cols(n)], 1, 0)))
        )
        pl.when(t < UNITS)(lambda: red.phase0(t))

        @pl.when(dense)
        def _():
            def tile(n):
                acc[:, cols(n)] = dot(wb[slot, 0], wb[slot, 1, :, cols(n)], 0, 0)
                grad_in[:, cols(n)] = jnp.zeros((LEN, 256), F32)

            tiles(tile)

        @pl.when(qkv)
        def _():
            ones = jnp.ones((8, LEN), BF)

            def tile(n):
                grad_in[:, cols(n)] += dot(wb[slot, 0], wb[slot, 1, cols(n), :], 0, 1)
                gv[pl.ds(t + 1, 1), cols(n)] = dot(ones, wb[slot, 0, cols(n), :], 1, 1)[:1]

            tiles(tile)

        @pl.when(expand)
        def _():
            def tile(n):
                acc[:, cols(n)] += dot(gelu[...], wb[slot, 0, :, cols(n)], 1, 0)
                grad_in[:, cols(n)] += dot(dact[...], wb[slot, 1, cols(n), :], 1, 1)

            tiles(tile)

        pl.when(t == UNITS)(finish)
        if fused:
            pl.when(t == UNITS)(vecs.stage0)
            pl.when(t == UNITS + 1)(vecs.stage1)

            @pl.when(t == UNITS + 2)
            def _():
                gtable[...] = vecs.stage2()

        return carry

    lax.fori_loop(0, UNITS + PHASES - 1, tick, 0)
    if fused:
        norm[...] = vecs.norm(wide[...], gtable[...])
    else:
        gtable[...] = gv[...]
        norm[...] = jnp.zeros((1, 1), F32)


def back(tokens, dy, ht, table, act, full, nz, reps):
    shards = 2 * nz
    count = Reduce.sems(nz)
    vcount = VecSum.sems(shards, reps)
    anywhere = pl.BlockSpec(memory_space=pl.ANY)
    inside = pl.BlockSpec(memory_space=pltpu.VMEM)

    def kernel(*refs):
        back_kernel(nz, reps, *refs)

    return pl.pallas_call(
        kernel,
        out_shape=(
            jax.ShapeDtypeStruct((LEN, D), BF),
            jax.ShapeDtypeStruct((LEN, D), F32),
            jax.ShapeDtypeStruct((UNITS, 4, 32, D), BF),
            jax.ShapeDtypeStruct((VPAD, 128 if reps == 4 else D), F32),
            jax.ShapeDtypeStruct((1, 1), F32),
        ),
        in_specs=[inside, inside, inside, inside, anywhere, anywhere],
        out_specs=(inside,) * 5,
        scratch_shapes=[
            pltpu.VMEM((2, 2, D, D), BF),
            pltpu.VMEM((2, nz, 2, 2, 2, 32, D), BF),
            pltpu.VMEM((RC, nz, 2, 2, 32, D), BF),
            pltpu.VMEM((UNITS, nz, 2, 32, D), BF),
            pltpu.VMEM((UNITS, nz, 32, D), BF),
            pltpu.VMEM((UNITS, nz - 1, 32, D), BF),
            pltpu.VMEM((LEN, D), BF),
            pltpu.VMEM((LEN, D), BF),
            pltpu.VMEM((LEN, D), F32),
            pltpu.VMEM((FF // D, D), F32),
            pltpu.VMEM((FF // D, D), F32),
            pltpu.VMEM((VPAD, D), F32),
            pltpu.VMEM((8, D), F32),
            pltpu.VMEM((shards, VPAD, 128), F32),
            pltpu.VMEM((reps, VPAD, 128), F32),
            pltpu.VMEM((shards, 8, 128), F32),
            pltpu.SemaphoreType.DMA((UNITS, count)),
            pltpu.SemaphoreType.DMA((UNITS, count)),
            pltpu.SemaphoreType.DMA((vcount,)),
            pltpu.SemaphoreType.DMA((vcount,)),
            pltpu.SemaphoreType.DMA((2, 2)),
        ],
        compiler_params=pltpu.CompilerParams(
            collective_id=1, has_side_effects=True, vmem_limit_bytes=60 * MIB
        ),
        name="back",
    )(tokens, dy, ht, table, act, full)


def norm_kernel(shards, reps, gvec, own, gtable, norm, v1, v2, sq, send, recv):
    vecs = VecSum(shards, reps, gvec, v1, v2, sq, send, recv)
    greet(vecs.row + vecs.col)
    vecs.stage0()
    wide = lax.fori_loop(
        0, own.shape[0], lambda u, acc: acc + fold_squares(own[u]), jnp.zeros((8, D), F32)
    )
    vecs.stage1()
    gtable[...] = vecs.stage2()
    norm[...] = vecs.norm(wide, gtable[...])


def norm_all(gvec, own, shards, reps):
    count = VecSum.sems(shards, reps)

    def kernel(*refs):
        norm_kernel(shards, reps, *refs)

    inside = pl.BlockSpec(memory_space=pltpu.VMEM)
    return pl.pallas_call(
        kernel,
        out_shape=(
            jax.ShapeDtypeStruct((VPAD, 128), F32),
            jax.ShapeDtypeStruct((1, 1), F32),
        ),
        in_specs=[inside, inside],
        out_specs=(inside, inside),
        scratch_shapes=[
            pltpu.VMEM((shards, VPAD, 128), F32),
            pltpu.VMEM((reps, VPAD, 128), F32),
            pltpu.VMEM((shards, 8, 128), F32),
            pltpu.SemaphoreType.DMA((count,)),
            pltpu.SemaphoreType.DMA((count,)),
        ],
        compiler_params=pltpu.CompilerParams(
            collective_id=2, has_side_effects=True, vmem_limit_bytes=56 * MIB
        ),
        name="norm_all",
    )(gvec, own)


def adamw(master, firsts, seconds, gradient, factor, step_rate, decay_amount):
    clipped = gradient * factor
    momentum = 0.9 * firsts + 0.1 * clipped
    variance = 0.95 * seconds + 0.05 * clipped * clipped
    corrected = momentum / (1.0 - 0.9**STEP)
    spread = variance / (1.0 - 0.95**STEP)
    renewed = master - step_rate * (corrected / (jnp.sqrt(spread) + 1e-08) + decay_amount * master)
    return (momentum, variance, renewed)


def update_kernel(shards, norm, own, own_shrink, *refs):
    ins, outs = refs[:12], refs[12:]
    factor = jnp.minimum(1.0, clip_limit / (norm[...] + 1e-06))
    width = FF // shards

    def part(number, rows, lanes, gradient):
        trio = ins[3 * number : 3 * number + 3]
        new = adamw(
            *(ref[rows, lanes] for ref in trio), gradient.astype(F32), factor, matrix_rate, decay_rate
        )
        for ref, value in zip(outs[3 * number : 3 * number + 3], new):
            ref[rows, lanes] = value

    every = slice(None)
    for i in range(3):
        part(0, every, slice(i * D, i * D + D), own[1 + i])
    part(1, every, every, own[0])
    for j in range(FF // D):
        for s in range(shards):
            f = s * width + j * 128
            part(2, every, slice(f, f + 128), own[5 + 2 * j, :, s * 128 : s * 128 + 128])
    part(3, every, every, own_shrink[0])


def update_all(norm, own, states, shards):
    steps = 8
    rows = 128 // steps
    specs = []
    for master in states[::3]:
        height, lanes = master.shape
        specs += [pl.BlockSpec((height // steps, lanes), lambda i: (i, 0))] * 3

    def kernel(*refs):
        update_kernel(shards, *refs)

    return pl.pallas_call(
        kernel,
        grid=(steps,),
        out_shape=tuple(jax.ShapeDtypeStruct(a.shape, F32) for a in states),
        in_specs=[
            pl.BlockSpec((1, 1), lambda i: (0, 0)),
            pl.BlockSpec((UNITS, rows, D), lambda i: (0, i, 0)),
            pl.BlockSpec((1, 4 * rows, D), lambda i: (4 + 2 * (i // 2), i % 2, 0)),
        ]
        + specs,
        out_specs=tuple(specs),
        compiler_params=pltpu.CompilerParams(vmem_limit_bytes=56 * MIB),
        name="update",
    )(norm, own, own, *states)


def body(
    tokens,
    doc_lengths,
    cotangent,
    qkv_weight,
    qkv_firsts,
    qkv_seconds,
    dense_weight,
    dense_firsts,
    dense_seconds,
    expand_weight,
    expand_firsts,
    expand_seconds,
    shrink_weight,
    shrink_firsts,
    shrink_seconds,
    vectors,
    vec_firsts,
    vec_seconds,
    *,
    shards,
    reps,
):
    nz = shards // 2
    vec_own = jnp.pad(vectors.astype(BF).T, ((0, VPAD - VROWS), (0, 0)))
    full, table, ht, act = front(
        doc_lengths, tokens, cotangent, qkv_weight, dense_weight, vec_own, expand_weight, shrink_weight, nz
    )
    output, grad_in, owned, gtable, norm = back(
        tokens, cotangent, ht, table, act, full.reshape(UNITS, D, D), nz, reps
    )
    owned = owned.reshape(UNITS, 128, D)
    if reps != 4:
        quads = [[4 * i + j for i in range(reps // 4)] for j in range(4)]
        owned = lax.psum(owned, "rep", axis_index_groups=quads)
        gtable, norm = norm_all(gtable, owned, shards, reps)
    states = (
        qkv_weight, qkv_firsts, qkv_seconds,
        dense_weight, dense_firsts, dense_seconds,
        expand_weight, expand_firsts, expand_seconds,
        shrink_weight, shrink_firsts, shrink_seconds,
    )
    updates = []
    new = update_all(norm, owned, states, shards)
    for i in range(4):
        renewed, momentum, variance = 3 * i + 2, 3 * i, 3 * i + 1
        updates += [new[momentum], new[variance], new[renewed]]
    grad_norm = norm.reshape(1)
    factor = jnp.minimum(1.0, clip_limit / (grad_norm + 1e-06))
    updates += adamw(
        vectors, vec_firsts, vec_seconds, gtable[:VROWS].T, factor, vector_rate, 0.0
    )
    return (output, grad_in) + tuple(updates) + (grad_norm,)


def solution(mesh):
    shards, reps = mesh.shape["shard"], mesh.shape["rep"]
    data, state = P(("rep", "shard"), None), P("shard", None)

    def step(*args):
        return body(*args, shards=shards, reps=reps)

    return jax.shard_map(
        step,
        mesh=mesh,
        in_specs=(data, data, data) + (state,) * 15,
        out_specs=(data, data) + (state,) * 15 + (P(),),
        check_vma=False,
    )
```

time: 1110 us -> 375 us (0.34)
  waiting for transfers between devices: 561 us -> 0 us
  Pallas kernels: 0 us -> 364 us
  matrix products: 293 us -> 0 us
  other arithmetic: 136 us -> 2.03 us
  blocking collectives: 55.9 us -> 0 us
  local copies, waits for them, and re-layouts: 42.5 us -> 5.57 us
  between operations: 20.4 us -> 3.18 us
    pallas_call x0 -> x3, Pallas kernels: none -> 364 us  [the longest x1 192 us: back(): pl.pallas_call(kernel, out_shape=(jax.ShapeDtypeStruct((LEN, D), BF), jax...]
    reduce_scatter x4 -> x0, waiting for transfers between devices: 344 us -> none  [the longest x1 152 us: body(): lax.psum_scatter(local_grads[3].astype(jnp.bfloat16), 'shard', scatter_di...]
    dot_general x24 -> x0, matrix products: 293 us -> none  [the longest x2 37.2 us: attend_backward(): jnp.einsum('qhd,khd->hqk', rows_grad, seq_values[:key_stop], preferred_el...]
    all_gather x4 -> x0, waiting for transfers between devices: 108 us -> none  [body(): lax.all_gather(shortened(shards), 'shard', axis=0, tiled=True)]
    psum x1 -> x0, waiting for transfers between devices: 63.4 us -> none  [body(): lax.psum(owned[1].astype(jnp.bfloat16), 'rep').astype(jnp.float32)]
    convert_element_type x10 -> x0, other arithmetic: 51 us -> none  [the longest x2 40.6 us: attend_backward(): grad_scores = (probs * (grad_probs - inner)).astype(jnp.bfloat16)]
    unnamed x11 -> x0, waiting for transfers between devices: 45.4 us -> none
    reduce_sum x13 -> x0, other arithmetic: 43.4 us -> none  [the longest x2 23.8 us: attend_forward(): totals = jnp.sum(weights, axis=-1, keepdims=True)]
  transfers between devices with their start and end apart: 10 -> 0, of which waited for: 7 -> 0; matrix products, arithmetic and copies ran while one was open for 38% -> 0% of each run, Pallas kernels for 0% -> 0%
where the time goes in v1:
time: 375 us; the launch traced here: 374 us
  Pallas kernels  364 us (97%)
  local copies, waits for them, and re-layouts  5.57 us (1%)
    pallas_call x1, Pallas kernels, back(): pl.pallas_call(kernel, out_shape=(jax.ShapeDtypeStruct((LEN, D), BF), jax...  192 us
    pallas_call x1, Pallas kernels, front(): pl.pallas_call(kernel, out_shape=(jax.ShapeDtypeStruct((UNITS, shards, 12...  155 us
    pallas_call x1, Pallas kernels, update_all(): pl.pallas_call(kernel, grid=(steps,), out_shape=tuple((jax.ShapeDtypeStru...  16.7 us

profile of v1, /device:TPU:0, one launch (start us, length us, event | category | flops | bytes accessed | tf_op | source)
XLA Modules:
  0.0 374.4 jit_solution(8567604440510635456)
XLA Ops:
  0.7 0.7 convert_bitcast_fusion
  1.4 0.6 pad.4.refs_5_
  2.0 155.1 %front.1 = (bf16[12,8,128,1024]{3,2,1,0:T(8,128)(2,1)}, bf16[16,1024]{1,0:T(8,128)(2,1)}, bf16[1024,1024]{1,0:T(8,128)(2,1)}, bf16[4,1024,1024]{2,1,0:T(8,128)(2,1)}) custom-call(s32[1,4]{1,0:T(1,128)} %refs_0_.2, bf16[1024,1024]{1,0:T(8,128)(2,1)} %refs_0_.3, bf16[1024,1024]{1,0:T(8,128)(2,1)} %refs_1_.3, f32[128,3072]{1,0:T(8,128)} %refs_3_.3, ...), custom_call_target="tpu_custom_call" | custom-call | tf_op jit(solution)/shard_map/front/pallas_call | solution.py:441
  157.1 0.0 copy-start.2
  157.1 0.0 copy-start.3
  157.1 0.0 copy-start.4
  157.1 191.8 %back.1 = (bf16[1024,1024]{1,0:T(8,128)(2,1)}, f32[1024,1024]{1,0:T(8,128)}, bf16[12,4,32,1024]{3,2,1,0:T(8,128)(2,1)}, f32[16,128]{1,0:T(8,128)}, f32[1,1]{1,0:T(1,128)}) custom-call(bf16[1024,1024]{1,0:T(8,128)(2,1)} %refs_0_.3, bf16[1024,1024]{1,0:T(8,128)(2,1)} %refs_1_.3, bf16[1024,1024]{1,0:T(8,128)(2,1)} %get-tuple-element.39.refs_2_, ...), custom_call_target="tpu_custom_call" | custom-call | tf_op jit(solution)/shard_map/back/pallas_call | solution.py:865
  349.6 0.0 copy-done.2
  349.6 0.0 copy-done.3
  349.7 0.0 copy-done.4
  349.7 1.3 multiply_subtract_fusion
  351.0 0.0 copy-start.1
  351.0 16.7 %update.1 = (f32[128,3072]{1,0:T(8,128)}, f32[128,3072]{1,0:T(8,128)}, f32[128,3072]{1,0:T(8,128)}, f32[128,1024]{1,0:T(8,128)}, f32[128,1024]{1,0:T(8,128)}, /*...) custom-call(f32[1,1]{1,0:T(1,128)} %get-tuple-element.45.refs_0_, ...), custom_call_target="tpu_custom_call" | custom-call | tf_op jit(solution)/shard_map/update/pallas_call | solution.py:992
  367.7 0.0 copy-done.1
  367.7 0.0 copy-start
  367.7 1.3 copy.39
  369.1 1.6 copy-done
  370.7 2.0 copy.40
Async XLA Ops:
  157.1 192.5 %copy-start.2 = (f32[128,11]{0,1:T(8,128)S(1)}, f32[128,11]{0,1:T(8,128)}, u32[]{:S(2)}) copy-start(f32[128,11]{0,1:T(8,128)} %param.33) | copy-start | bytes 16900
  157.1 192.5 %copy-start.3 = (f32[128,11]{0,1:T(8,128)S(1)}, f32[128,11]{0,1:T(8,128)}, u32[]{:S(2)}) copy-start(f32[128,11]{0,1:T(8,128)} %param.35) | copy-start | bytes 16900
  157.1 192.5 %copy-start.4 = (f32[128,11]{0,1:T(8,128)S(1)}, f32[128,11]{0,1:T(8,128)}, u32[]{:S(2)}) copy-start(f32[128,11]{0,1:T(8,128)} %param.34) | copy-start | bytes 16900
  351.0 16.7 %copy-start.1 = (bf16[1024,1024]{1,0:T(8,128)(2,1)S(1)}, bf16[1024,1024]{1,0:T(8,128)(2,1)}, u32[]{:S(2)}) copy-start(bf16[1024,1024]{1,0:T(8,128)(2,1)} %get-tuple-element.81) | copy-start | bytes 6291460
  367.7 2.9 copy-start

commit v2 on v1

v2 whole, which is shorter than its diff:
```python
import math

import jax
import jax.numpy as jnp
from jax import lax
from jax.experimental import pallas as pl
from jax.experimental.pallas import tpu as pltpu
from jax.sharding import PartitionSpec as P

D = 1024
HEADS = 16
HEAD_DIM = 64
ROTARY = 32
FF = 4096
LEN = 1024
STEP = 10
VROWS = 11
VPAD = 16
UNITS = 12
QB = 256

clip_limit = 1.0
matrix_rate = 0.05
vector_rate = 0.8
decay_rate = 0.1

BF = jnp.bfloat16
F32 = jnp.float32
MIB = 1 << 20


def dot(a, b, ca, cb):
    return lax.dot_general(a, b, (((ca,), (cb,)), ((), ())), preferred_element_type=F32)


class Place:
    def __init__(self, nz):
        self.nz = nz
        self.r = lax.axis_index("rep")
        self.s = lax.axis_index("shard")
        self.z, self.x = self.s // 2, self.s % 2
        self.c = self.r % 2
        self.y = (self.r // 2) % 2
        self.p = 2 * self.c + self.y

    def dev(self, r, s):
        return {"rep": r, "shard": s}

    def zpeer(self, k):
        return self.dev(self.r, ((self.z + k) % self.nz) * 2 + self.x)

    @property
    def xpeer(self):
        return self.dev(self.r, self.z * 2 + 1 - self.x)

    @property
    def ypeer(self):
        return self.dev(self.r + 2 - 4 * self.y, self.s)

    @property
    def cpeer(self):
        return self.dev(self.r + 1 - 2 * self.c, self.s)

    @property
    def diag(self):
        return self.dev(self.r + 2 - 4 * self.y + 1 - 2 * self.c, self.s)

    def swap(self, first):
        on_x = self.c == (0 if first else 1)
        return self.dev(
            jnp.where(on_x, self.r, self.r + 2 - 4 * self.y),
            jnp.where(on_x, self.z * 2 + 1 - self.x, self.s),
        )


def greet(peers):
    barrier = pltpu.get_barrier_semaphore()
    for peer in peers:
        pl.semaphore_signal(barrier, inc=1, device_id=peer, device_id_type=pl.DeviceIdType.MESH)
    pl.semaphore_wait(barrier, len(peers))


def remote(src, dst, send, recv, peer):
    return pltpu.make_async_remote_copy(
        src_ref=src,
        dst_ref=dst,
        send_sem=send,
        recv_sem=recv,
        device_id=peer,
        device_id_type=pl.DeviceIdType.MESH,
    )


class Gather:
    STAGES = 5

    def __init__(self, at, own, full, u0, n, lane, width, send, recv, job):
        self.at, self.own, self.full = at, own, full
        self.us, self.lanes = pl.ds(u0, n), pl.ds(lane, width)
        self.send, self.recv, self.job = send, recv, job

    def rows(self, count):
        at = self.at
        return pl.ds(at.c * 64 + at.y * 32, 32) if count == 32 else pl.ds(at.c * 64, 64)

    def part(self, z, x, rows):
        return self.full.at[self.us, z, x, rows, self.lanes]

    def copy(self, i, src, dst, peer):
        return remote(src, dst, self.send.at[self.job, i], self.recv.at[self.job, i], peer)

    def all_of(self, i):
        every = slice(None)
        z, x, count = ((pl.ds(0, self.at.nz - 1), 0, 32), (every, 0, 32), (every, every, 32), (every, every, 64))[i]
        ref = self.part(z, x, pl.ds(0, count))
        return self.copy(i, ref, ref, self.at.cpeer)

    def stage0(self):
        at = self.at
        src = self.own.at[self.us, self.rows(32), self.lanes]
        for k in range(1, at.nz):
            self.copy(0, src, self.part(at.z, at.x, self.rows(32)), at.zpeer(k)).start()

    def stage1(self):
        self.all_of(0).wait_recv()
        ref = self.part(slice(None), self.at.x, self.rows(32))
        self.copy(1, ref, ref, self.at.swap(True)).start()

    def stage2(self):
        at = self.at
        self.all_of(1).wait_recv()
        along_y = self.part(slice(None), slice(None), self.rows(32))
        along_x = self.part(slice(None), at.x, self.rows(64))
        pl.when(at.c == 0)(lambda: self.copy(2, along_y, along_y, at.ypeer).start())
        pl.when(at.c == 1)(lambda: self.copy(2, along_x, along_x, at.xpeer).start())

    def stage3(self):
        self.all_of(2).wait_recv()
        ref = self.part(slice(None), slice(None), self.rows(64))
        self.copy(3, ref, ref, self.at.cpeer).start()

    def stage4(self):
        self.all_of(3).wait_recv()
        for i in range(4):
            self.all_of(i).wait_send()


def rotate_rows(u, cosine, sine):
    top = u[:16] * cosine - u[16:32] * sine
    low = u[16:32] * cosine + u[:16] * sine
    return jnp.concatenate([top, low, u[32:]], axis=0)


def heads_attention(base, bias, qt, kt, vt, gt, act, dqt, dkt, dvt, pause):
    def scores(head, number):
        q0 = number * QB
        k0 = max(0, number - 2) * QB
        span = q0 + QB - k0
        rows = slice(64 * head, 64 * head + 64)
        q, g = qt[rows, q0 : q0 + QB], gt[rows, q0 : q0 + QB]
        k, v = kt[rows, k0 : k0 + span], vt[rows, k0 : k0 + span]
        return q, g, k, v, dot(k, q, 0, 0) + bias[number, :span], dot(v, g, 0, 0)

    def weigh(head, number, q, g, k, v, s, dp):
        outs = pl.ds(pl.multiple_of(base + 64 * head, 64), 64)
        e = jnp.exp(s - jnp.max(s, axis=0, keepdims=True))
        p = e * (1.0 / jnp.sum(e, axis=0, keepdims=True))
        pb = p.astype(BF)
        o = dot(v, pb, 1, 0)
        inner = jnp.sum(o * g.astype(F32), axis=0, keepdims=True)
        ds = (p * (dp - inner)).astype(BF)
        act[0, outs, number * QB : number * QB + QB] = o.astype(BF)
        return q, g, k, pb, ds

    def spread(head, number, q, g, k, pb, ds):
        q0 = number * QB
        k0 = max(0, number - 2) * QB
        old = q0 - k0
        rows = slice(64 * head, 64 * head + 64)
        dqt[rows, q0 : q0 + QB] = dot(k, ds, 1, 0)
        dk = dot(q, ds, 1, 1)
        dv = dot(g, pb, 1, 1)
        if old:
            dkt[rows, k0:q0] += dk[:, :old]
            dvt[rows, k0:q0] += dv[:, :old]
        dkt[rows, q0 : q0 + QB] = dk[:, old:]
        dvt[rows, q0 : q0 + QB] = dv[:, old:]

    order = [(head, number) for number in range(LEN // QB) for head in range(4)]
    ready, waiting = scores(*order[0]), None
    for i, (head, number) in enumerate(order):
        following = scores(*order[i + 1]) if i + 1 < len(order) else None
        weighed = weigh(head, number, *ready)
        if waiting is not None:
            spread(*waiting)
        waiting, ready = (head, number, *weighed), following
        if i % 4 == 3:
            pause(i // 4)
    spread(*waiting)


JOBS = UNITS + 1
READY = 6
LAGS = (0, 2, 3, 5, 6)


def run_stage(gather, stage):
    getattr(gather, f"stage{stage}")()


def front_kernel(
    nz,
    lengths, tokens, dy, wqkv, wd, vec, wexpand, wshrink,
    full, table, ht, act,
    own, expand_f, shrink_f, wd_v, wq_v, bias, cosine, sine, qt, kt, vt, gt, dqf, dkf, dvf,
    send, recv, vsend, vrecv, lsem,
):
    at = Place(nz)
    shards = 2 * nz
    others = [at.dev(at.r, (at.s + k) % shards) for k in range(1, shards)]
    load_expand = pltpu.make_async_copy(wexpand, expand_f, lsem.at[0])
    load_shrink = pltpu.make_async_copy(wshrink, shrink_f, lsem.at[1])
    load_expand.start()
    load_shrink.start()
    own[0] = wd[...].astype(BF)
    for i in range(3):
        own[1 + i] = wqkv[:, i * D : i * D + D].astype(BF)
    greet(others + [at.ypeer, at.cpeer])

    def lanes(i):
        return pl.ds(pl.multiple_of(i * 128, 128), 128)

    vcopies = [
        remote(vec, table.at[:, lanes(at.s)], vsend.at[k], vrecv.at[k], peer)
        for k, peer in enumerate(others)
    ]
    for copy in vcopies:
        copy.start()
    table[:, lanes(at.s)] = vec[...]
    mine = pl.ds(at.p * 32, 32)
    local_a = pltpu.make_async_copy(
        own.at[0:4, mine], full.at[0:4, at.z, at.x, mine], lsem.at[2]
    )
    local_a.start()
    local_f = pltpu.make_async_copy(
        own.at[4:UNITS, mine], full.at[4:UNITS, at.z, at.x, mine], lsem.at[3]
    )

    def cast_rest():
        load_expand.wait()
        load_shrink.wait()
        width = FF // shards
        for j in range(FF // D):
            own[4 + 2 * j] = shrink_f[j * 128 : j * 128 + 128].astype(BF)
            for b in range(shards):
                own[5 + 2 * j, :, b * 128 : b * 128 + 128] = expand_f[
                    :, b * width + j * 128 : b * width + j * 128 + 128
                ].astype(BF)
        local_f.start()

    def tables():
        place = lax.broadcasted_iota(jnp.int32, (1, LEN), 1)
        start = jnp.zeros((1, LEN), jnp.int32)
        end = 0
        for d in range(lengths.shape[1]):
            end = end + lengths[0, d]
            start = start + jnp.where(place >= end, lengths[0, d], 0)
        m = lax.broadcasted_iota(jnp.int32, (ROTARY // 2, LEN), 0).astype(F32)
        frequency = jnp.exp(m * (-2.0 * math.log(10000.0) / ROTARY))
        angle = (place - start).astype(F32) * frequency
        cosine[...] = jnp.cos(angle)
        sine[...] = jnp.sin(angle)
        for number in range(LEN // QB):
            q0 = number * QB
            k0 = max(0, number - 2) * QB
            span = q0 + QB - k0
            j = k0 + lax.broadcasted_iota(jnp.int32, (span, QB), 0)
            i = q0 + lax.broadcasted_iota(jnp.int32, (span, QB), 1)
            allowed = (j >= start[:, q0 : q0 + QB]) & (j <= i)
            bias[number, :span] = jnp.where(allowed, 0.0, -1e30)

    def wait_vec():
        for k, copy in enumerate(vcopies):
            came = (at.s + shards - (k + 1)) % shards
            remote(vec, table.at[:, lanes(came)], vsend.at[k], vrecv.at[k], others[k]).wait_recv()
            copy.wait_send()

    def norm_rows(i):
        rows = pl.ds(pl.multiple_of(i * 256, 256), 256)
        x = tokens[rows].astype(F32)
        centered = x - jnp.mean(x, axis=1, keepdims=True)
        scaled = centered * lax.rsqrt(jnp.mean(centered * centered, axis=1, keepdims=True) + 1e-05)
        h = scaled * table[0:1].astype(F32) + table[1:2].astype(F32)
        ht[:, rows] = h.astype(BF).T

    def part(job, stage):
        args = (send, recv, job)
        if isinstance(job, int):
            if job == 1:
                gather = Gather(at, own, full, 0, 1, 0, D, *args)
            elif job < 5:
                gather = Gather(at, own, full, 1, 3, 256 * max(0, job - 1), 256, *args)
            else:
                gather = Gather(at, own, full, job - 1, 1, 0, D, *args)
            run_stage(gather, stage)
            return
        lane = pl.multiple_of((job - 1) * 256, 256)
        pl.when((job >= 2) & (job < 5))(
            lambda: run_stage(Gather(at, own, full, 1, 3, lane, 256, *args), stage)
        )
        pl.when((job >= 5) & (job < JOBS))(
            lambda: run_stage(Gather(at, own, full, job - 1, 1, 0, D, *args), stage)
        )

    def load_quad(quad):
        lane = quad * 256 if isinstance(quad, int) else pl.multiple_of(quad * 256, 256)
        src = full.at[pl.ds(1, 3), :, :, :, pl.ds(lane, 256)]
        return pltpu.make_async_copy(src, wq_v.at[quad % 2], lsem.at[4 + quad % 2])

    load_dense = pltpu.make_async_copy(full.at[0], wd_v, lsem.at[6])
    side = {
        0: (tables,),
        1: (wait_vec, lambda: norm_rows(0)),
        2: (lambda: norm_rows(1), lambda: norm_rows(2)),
        3: (lambda: norm_rows(3),),
        4: (cast_rest,),
    }
    for step in range(READY):
        for stage in range(Gather.STAGES):
            if 0 <= step - stage < 2:
                if step == 1 and stage == 1:
                    local_a.wait()
                part(step - stage, stage)
            if step - LAGS[stage] >= 2:
                part(step - LAGS[stage], stage)
        for what in side.get(step, ()):
            what()
        if step == 4:
            load_quad(0).start()
    load_dense.start()
    local_f.wait()

    def prepare(quad):
        cols = pl.ds(pl.multiple_of(quad * 256, 256), 256)
        load_quad(quad).wait()
        pl.when(quad == 0)(load_dense.wait)
        for part, dst in enumerate((qt, kt, vt)):
            w = wq_v[quad % 2, part].reshape(D, 256)
            u = dot(w, ht[...], 0, 0)
            ones = jnp.ones((1, 128), BF)
            b = dot(table[2 + part : 3 + part, cols], ones, 0, 0)[:, :1]
            u = u + b
            if part == 2:
                dst[...] = u.astype(BF)
                continue
            for head in range(4):
                turned = rotate_rows(u[head * 64 : head * 64 + 64], cosine[...], sine[...])
                if part == 0:
                    turned = turned * (1.0 / math.sqrt(HEAD_DIM))
                dst[head * 64 : head * 64 + 64] = turned.astype(BF)
        for half in range(2):
            w = wd_v[quad, half]
            gt[half * 128 : half * 128 + 128] = dot(w, dy[...], 1, 1).astype(BF)

    def one_quad(quad, carry):
        prepare(quad)
        base = quad * 256

        def pause(number):
            i, left = quad * 4 + number, JOBS + LAGS[-1] - READY
            before, after = ((n * left + HEADS - 1) // HEADS for n in (i, i + 1))

            @pl.when(after > before)
            def _():
                for stage, lag in enumerate(LAGS):
                    part(READY + before - lag, stage)

            if number == 2:
                pl.when(quad < 3)(lambda: load_quad(quad + 1).start())

        heads_attention(base, bias, qt, kt, vt, gt, act, dqf, dkf, dvf, pause)
        for head in range(4):
            rows = slice(64 * head, 64 * head + 64)
            outs = pl.ds(pl.multiple_of(base + 64 * head, 64), 64)
            back = rotate_rows(dqf[rows], cosine[...], -sine[...]) * (1.0 / math.sqrt(HEAD_DIM))
            act[1, outs] = back.astype(BF)
            act[2, outs] = rotate_rows(dkf[rows], cosine[...], -sine[...]).astype(BF)
            act[3, outs] = dvf[rows].astype(BF)
        return carry

    lax.fori_loop(0, 4, one_quad, 0)


def front(lengths, tokens, dy, wqkv, wd, vec, wexpand, wshrink, nz):
    shards = 2 * nz
    anywhere = pl.BlockSpec(memory_space=pl.ANY)
    inside = pl.BlockSpec(memory_space=pltpu.VMEM)

    def kernel(*refs):
        front_kernel(nz, *refs)

    return pl.pallas_call(
        kernel,
        out_shape=(
            jax.ShapeDtypeStruct((UNITS, nz, 2, 128, D), BF),
            jax.ShapeDtypeStruct((VPAD, D), BF),
            jax.ShapeDtypeStruct((D, LEN), BF),
            jax.ShapeDtypeStruct((4, D, LEN), BF),
        ),
        in_specs=[
            pl.BlockSpec(memory_space=pltpu.SMEM),
            inside,
            inside,
            inside,
            inside,
            inside,
            anywhere,
            anywhere,
        ],
        out_specs=(anywhere, inside, inside, inside),
        scratch_shapes=[
            pltpu.VMEM((UNITS, 128, D), BF),
            pltpu.VMEM(wexpand.shape, F32),
            pltpu.VMEM(wshrink.shape, F32),
            pltpu.VMEM((nz, 2, 128, D), BF),
            pltpu.VMEM((2, 3, nz, 2, 128, 256), BF),
            pltpu.VMEM((LEN // QB, 3 * QB, QB), F32),
            pltpu.VMEM((ROTARY // 2, LEN), F32),
            pltpu.VMEM((ROTARY // 2, LEN), F32),
            pltpu.VMEM((256, LEN), BF),
            pltpu.VMEM((256, LEN), BF),
            pltpu.VMEM((256, LEN), BF),
            pltpu.VMEM((256, LEN), BF),
            pltpu.VMEM((256, LEN), F32),
            pltpu.VMEM((256, LEN), F32),
            pltpu.VMEM((256, LEN), F32),
            pltpu.SemaphoreType.DMA((JOBS, 4)),
            pltpu.SemaphoreType.DMA((JOBS, 4)),
            pltpu.SemaphoreType.DMA((shards - 1,)),
            pltpu.SemaphoreType.DMA((shards - 1,)),
            pltpu.SemaphoreType.DMA((8,)),
        ],
        compiler_params=pltpu.CompilerParams(
            collective_id=0, has_side_effects=True, vmem_limit_bytes=58 * MIB
        ),
        name="front",
    )(lengths, tokens, dy, wqkv, wd, vec, wexpand, wshrink)


RC, RB = 3, 6


class Reduce:
    def __init__(self, at, grads, rc, rb, ra, rz, out, send, recv):
        self.at = at
        self.grads, self.rc, self.rb, self.ra, self.rz, self.out = grads, rc, rb, ra, rz, out
        self.send, self.recv = send, recv

    SEMS = 6

    def copy(self, u, i, src, dst, peer):
        send = self.send.at[u, i] if i < 3 else self.send.at[UNITS, i]
        return remote(src, dst, send, self.recv.at[u, i], peer)

    def finish(self):
        pieces = self.out.at[:, pl.ds(0, 1)], self.out.at[:, pl.ds(0, 2)]
        for i, ref in enumerate((self.rz,) + pieces):
            remote(ref, ref, self.send.at[UNITS, 3 + i], self.recv.at[0, 3 + i], self.at.cpeer).wait_send()

    def c(self, u):
        at = self.at
        return self.copy(u, 0, self.grads.at[u % 2, :, :, 1 - at.c], self.rc.at[u % RC], at.cpeer)

    def on_x(self, u):
        return (self.at.c == 1) | (u % 4 == 3)

    def b(self, u, on_x):
        at = self.at
        rc = self.rc.at[u % RC]
        src = rc.at[:, 1 - at.x] if on_x else rc.at[:, :, 1 - at.y]
        return self.copy(u, 1, src, self.rb.at[u % RB], at.xpeer if on_x else at.ypeer)

    def a(self, u, on_x):
        at = self.at
        src = self.rb.at[u % RB, :, 1 - (at.y if on_x else at.x)]
        return self.copy(u, 2, src, self.ra.at[u], at.ypeer if on_x else at.xpeer)

    def z(self, u, k):
        at = self.at
        src = self.ra.at[u, (at.z + k) % at.nz]
        return self.copy(u, 3, src, self.rz.at[u, k - 1], at.zpeer(k))

    def f(self, u):
        ref = self.out.at[u, self.at.p]
        return self.copy(u, 4, ref, ref, self.at.ypeer)

    def f_in(self, u):
        ref = self.out.at[u, 2 * self.at.c + 1 - self.at.y]
        return self.copy(u, 4, ref, ref, self.at.ypeer)

    def g(self, u):
        ref = self.out.at[u, pl.ds(2 * self.at.c, 2)]
        return self.copy(u, 5, ref, ref, self.at.cpeer)

    def g_in(self, u):
        ref = self.out.at[u, pl.ds(2 - 2 * self.at.c, 2)]
        return self.copy(u, 5, ref, ref, self.at.cpeer)

    def either(self, u, what):
        on_x = self.on_x(u)
        pl.when(on_x)(lambda: what(True))
        pl.when(jnp.logical_not(on_x))(lambda: what(False))

    def phase0(self, u):
        self.c(u).start()

    def phase1(self, u):
        at = self.at
        self.c(u).wait_recv()
        add_into(self.rc.at[u % RC], self.grads.at[u % 2, :, :, at.c])
        self.either(u, lambda on_x: self.b(u, on_x).start())

    def phase2(self, u):
        at = self.at
        rc, rb = self.rc.at[u % RC], self.rb.at[u % RB]
        self.b(u, True).wait_recv()

        def add(on_x):
            add_into(rb, rc.at[:, at.x] if on_x else rc.at[:, :, at.y])
            self.a(u, on_x).start()

        self.either(u, add)
        self.b(u, True).wait_send()
        self.c(u).wait_send()

    def phase3(self, u):
        at = self.at
        self.a(u, True).wait_recv()
        turn = jnp.where(self.on_x(u), at.y, at.x)
        add_into(self.ra.at[u], self.rb.at[u % RB, :, turn])
        for k in range(1, at.nz):
            self.z(u, k).start()
        self.a(u, True).wait_send()

    def phase4(self, u):
        at = self.at
        total = self.ra[u, at.z].astype(F32)
        self.copy(u, 3, self.rz.at[u], self.rz.at[u], at.cpeer).wait_recv()
        for k in range(1, at.nz):
            total += self.rz[u, k - 1].astype(F32)
        self.out[u, at.p] = total.astype(BF)
        self.f(u).start()

    def phase5(self, u):
        self.f_in(u).wait_recv()
        self.g(u).start()

    def phase6(self, u):
        self.g_in(u).wait_recv()


PHASES = 7
OFFSETS = (0, 1, 2, 3, 4, 5, 6)


def add_into(dst, src):
    dst[...] = dst[...] + src[...]


class VecSum:
    def __init__(self, shards, reps, gvec, v1, v2, sq, send, recv):
        self.shards, self.reps = shards, reps
        self.r, self.s = lax.axis_index("rep"), lax.axis_index("shard")
        self.row = [{"rep": self.r, "shard": (self.s + k) % shards} for k in range(1, shards)]
        self.col = [{"rep": (self.r + k) % reps, "shard": self.s} for k in range(1, reps)]
        self.gvec, self.v1, self.v2, self.sq = gvec, v1, v2, sq
        self.send, self.recv = send, recv

    @staticmethod
    def sems(shards, reps):
        return 2 * (shards - 1) + reps - 1

    def lanes(self, i):
        return pl.ds(pl.multiple_of(i * 128, 128), 128)

    def copy(self, i, src, dst, peer):
        return remote(src, dst, self.send.at[i], self.recv.at[i], peer)

    def over_shards(self, k):
        src = self.gvec.at[:, self.lanes((self.s + k) % self.shards)]
        return self.copy(k - 1, src, self.v1.at[self.s], self.row[k - 1])

    def over_reps(self, k):
        ref = self.v2.at[self.r]
        return self.copy(self.shards + k - 2, ref, ref, self.col[k - 1])

    def squares(self, k):
        ref = self.sq.at[self.s]
        return self.copy(self.shards + self.reps + k - 3, ref, ref, self.row[k - 1])

    def total(self, ref, count):
        every = ref[0]
        for i in range(1, count):
            every += ref[i]
        return every

    def stage0(self):
        for k in range(1, self.shards):
            self.over_shards(k).start()
        self.v1[self.s] = self.gvec[:, self.lanes(self.s)]

    def stage1(self):
        for k in range(1, self.shards):
            dst = self.v1.at[(self.s + self.shards - k) % self.shards]
            self.copy(k - 1, dst, dst, self.row[k - 1]).wait_recv()
            self.over_shards(k).wait_send()
        self.v2[self.r] = self.total(self.v1, self.shards)
        for k in range(1, self.reps):
            self.over_reps(k).start()

    def stage2(self):
        for k in range(1, self.reps):
            dst = self.v2.at[(self.r + self.reps - k) % self.reps]
            self.copy(self.shards + k - 2, dst, dst, self.col[k - 1]).wait_recv()
            self.over_reps(k).wait_send()
        return self.total(self.v2, self.reps)

    def norm(self, wide, table):
        part = table[:8] * table[:8] + table[8:] * table[8:]
        for i in range(D // 128):
            part += wide[:, i * 128 : i * 128 + 128]
        self.sq[self.s] = part
        for k in range(1, self.shards):
            self.squares(k).start()
        for k in range(1, self.shards):
            i = self.shards + self.reps + k - 3
            dst = self.sq.at[(self.s + self.shards - k) % self.shards]
            self.copy(i, dst, dst, self.row[k - 1]).wait_recv()
            self.squares(k).wait_send()
        return jnp.sqrt(jnp.sum(self.total(self.sq, self.shards), keepdims=True))


def fold_squares(block):
    g = block.astype(F32)
    return jnp.sum((g * g).reshape(-1, 8, D), axis=0)


WIDE = 512


def cols(n, width=WIDE):
    return pl.ds(pl.multiple_of(n * width, width), width)


def tiles(run):
    def one(n, carry):
        run(n)
        return carry

    lax.fori_loop(0, D // WIDE, one, 0)


def back_kernel(
    nz, reps,
    tokens, dy, ht, table, act, full,
    out_hbm, grad_hbm, owned, gtable, norm,
    grad_in, wb, grads, rc, rb, ra, rz, gelu, dact, acc, b1, gb1, gv, wide, v1, v2, sq,
    send, recv, vsend, vrecv, wsem, osem,
):
    at = Place(nz)
    shards = 2 * nz
    fused = reps == 4
    width = FF // shards

    def load(slot, first, second):
        for i, src in enumerate((first, second)):
            pltpu.make_async_copy(src, wb.at[slot, i], wsem.at[slot, i]).start()

    def loaded(slot):
        for i in range(2):
            pltpu.make_async_copy(full.at[0], wb.at[slot, i], wsem.at[slot, i]).wait()

    def load_mlp(j):
        load((j + 2) % 3, full.at[4 + 2 * j], full.at[5 + 2 * j])

    load(0, act.at[0], full.at[0])
    load(2, full.at[4], full.at[5])
    load(1, act.at[1], full.at[1])
    out = wb.at[0, 1]
    out_copy = pltpu.make_async_copy(out, out_hbm, osem.at[0])
    grad_copy = pltpu.make_async_copy(grad_in, grad_hbm, osem.at[1])
    red = Reduce(at, grads, rc, rb, ra, rz, owned, send, recv)
    vecs = VecSum(shards, reps, gv, v1, v2, sq, vsend, vrecv)
    gv[...] = jnp.zeros((VPAD, D), F32)
    wide[...] = jnp.zeros((8, D), F32)
    grad_in[...] = jnp.zeros((LEN, D), F32)
    for j in range(FF // D):
        for s in range(shards):
            f = s * width + j * 128
            b1[j : j + 1, s * 128 : s * 128 + 128] = table[
                6 + f // D : 7 + f // D, f % D : f % D + 128
            ].astype(F32)
    greet(vecs.row + [at.ypeer, at.cpeer, at.diag])

    def write(u, n, value):
        grads[u % 2, :, :, :, :, :, cols(n)] = value.astype(BF).reshape(nz, 2, 2, 2, 32, WIDE)

    def activate(j, half):
        slot = (j + 2) % 3
        parts = [pl.ds(pl.multiple_of(half * 512 + n * 256, 256), 256) for n in range(2)]
        products = []
        for part in parts:
            a = dot(ht[...], wb[slot, 1, :, part], 0, 0)
            products.append((a, dot(dy[...], wb[slot, 0, part, :], 1, 1)))
        for part, (a, dg) in zip(parts, products):
            a = a + b1[pl.ds(j, 1), part]
            square = a * a
            t = jnp.tanh(a * (math.sqrt(2.0 / math.pi) + (math.sqrt(2.0 / math.pi) * 0.044715) * square))
            gate = 0.5 + 0.5 * t
            gelu[j % 2, :, part] = (a * gate).astype(BF)
            slope = gate + a * (1.0 - t * t) * (
                0.5 * math.sqrt(2.0 / math.pi) + (1.5 * 0.044715 * math.sqrt(2.0 / math.pi)) * square
            )
            da = (dg * slope).astype(BF)
            dact[j % 2, :, part] = da
            gb1[pl.ds(j, 1), part] = jnp.sum(da.astype(F32), axis=0, keepdims=True)

    def finish():
        gain = table[0:1].astype(F32)
        shift = table[5:6].astype(F32) + table[10:11].astype(F32)

        def rows_of(i, carry):
            rows = pl.ds(pl.multiple_of(i * 128, 128), 128)
            x = wb[0, 0, rows].astype(F32)
            out[rows] = (x + acc[rows] + shift).astype(BF)
            centered = x - jnp.mean(x, axis=1, keepdims=True)
            rstd = lax.rsqrt(jnp.mean(centered * centered, axis=1, keepdims=True) + 1e-05)
            n = centered * rstd
            dh = grad_in[rows]
            back = dy[rows].astype(F32)
            e = dh * gain
            grad_in[rows] = back + rstd * (
                e
                - jnp.mean(e, axis=1, keepdims=True)
                - n * jnp.mean(e * n, axis=1, keepdims=True)
            )
            gv[0:1] += jnp.sum(dh * n, axis=0, keepdims=True)
            gv[1:2] += jnp.sum(dh, axis=0, keepdims=True)
            gv[5:6] += jnp.sum(back, axis=0, keepdims=True)
            return carry

        lax.fori_loop(0, LEN // 128, rows_of, 0)
        gv[10:11] = gv[5:6]
        for j in range(FF // D):
            for s in range(shards):
                f = s * width + j * 128
                gv[6 + f // D : 7 + f // D, f % D : f % D + 128] = gb1[
                    j : j + 1, s * 128 : s * 128 + 128
                ]

    def tick(t, carry):
        for number in range(1, PHASES):
            u = t - OFFSETS[number]

            def phase(u=u, number=number):
                getattr(red, f"phase{number}")(u)
                if number == PHASES - 1 and fused:
                    wide[...] += fold_squares(owned[u])

            pl.when((u >= 0) & (u < UNITS))(phase)

        dense, qkv = t == 0, (t >= 1) & (t < 4)
        even, odd = t % 2 == 0, t % 2 == 1
        shrink, expand = (t >= 4) & (t < UNITS) & even, (t >= 4) & (t < UNITS) & odd
        again = (t >= 8) & (t < 11)
        slot = t % 2
        j = (t - 4) // 2

        pl.when(t < 4)(lambda: loaded(slot))
        pl.when(t == 1)(lambda: loaded(2))
        pl.when((t == 1) | (t == 2))(lambda: load(1 - slot, act.at[t + 1], full.at[t + 1]))
        pl.when((t == 3) | (t == 4))(lambda: load_mlp(t - 2))
        pl.when(t == 6)(lambda: load_mlp(3))
        pl.when(again)(lambda: load(0, act.at[t - 7], full.at[t - 7]))
        inputs = pltpu.make_async_copy(tokens, wb.at[0, 0], wsem.at[0, 0])
        pl.when(t == 11)(lambda: inputs.start())

        pl.when(dense)(
            lambda: tiles(lambda n: write(t, n, dot(wb[slot, 0], dy[:, cols(n)], 1, 0)))
        )
        pl.when(qkv)(
            lambda: tiles(lambda n: write(t, n, dot(ht[...], wb[slot, 0, cols(n), :], 1, 1)))
        )
        pl.when(shrink)(
            lambda: tiles(lambda n: write(t, n, dot(gelu[j % 2], dy[:, cols(n)], 0, 0)))
        )
        pl.when(expand)(
            lambda: tiles(
                lambda n: write(t, n, dot(ht[...], dact[j % 2, :, cols(n)], 1, 0))
            )
        )
        pl.when(t < UNITS)(lambda: red.phase0(t))

        @pl.when(dense)
        def _():
            def tile(n):
                acc[:, cols(n)] = dot(wb[slot, 0], wb[slot, 1, :, cols(n)], 0, 0)

            tiles(tile)

        ends = (t == UNITS) | (t == UNITS + 1)
        of = jnp.where(ends, t - UNITS + 2, j)

        @pl.when((shrink & (t < 8)) | ends)
        def _():
            def tile(n):
                acc[:, cols(n)] += dot(gelu[of % 2], wb[(of + 2) % 3, 0, :, cols(n)], 1, 0)

            tiles(tile)

        @pl.when((expand & (t < 8)) | ends)
        def _():
            def tile(n):
                grad_in[:, cols(n)] += dot(
                    dact[of % 2], wb[(of + 2) % 3, 1, cols(n), :], 1, 1
                )

            tiles(tile)

        pl.when((t == 3) | (t == 5) | (t == 7))(lambda: loaded((t // 2 + 2) % 3))
        pl.when((t >= 1) & (t < 9))(lambda: activate((t - 1) // 2, 1 - t % 2))

        @pl.when(again)
        def _():
            loaded(0)
            ones = jnp.ones((8, LEN), BF)

            def tile(n):
                grad_in[:, cols(n)] += dot(wb[0, 0], wb[0, 1, cols(n), :], 0, 1)
                gv[pl.ds(t - 6, 1), cols(n)] = dot(ones, wb[0, 0, cols(n), :], 1, 1)[:1]

            tiles(tile)

        @pl.when(t == UNITS + 2)
        def _():
            inputs.wait()
            finish()
            out_copy.start()
            grad_copy.start()

        if fused:
            pl.when(t == UNITS + 3)(vecs.stage0)
            pl.when(t == UNITS + 4)(vecs.stage1)

            @pl.when(t == UNITS + 5)
            def _():
                gtable[...] = vecs.stage2()

        return carry

    lax.fori_loop(0, UNITS + OFFSETS[-1], tick, 0)
    red.finish()
    out_copy.wait()
    grad_copy.wait()
    if fused:
        norm[...] = vecs.norm(wide[...], gtable[...])
    else:
        gtable[...] = gv[...]
        norm[...] = jnp.zeros((1, 1), F32)


def back(tokens, dy, ht, table, act, full, nz, reps):
    shards = 2 * nz
    vcount = VecSum.sems(shards, reps)
    anywhere = pl.BlockSpec(memory_space=pl.ANY)
    inside = pl.BlockSpec(memory_space=pltpu.VMEM)

    def kernel(*refs):
        back_kernel(nz, reps, *refs)

    return pl.pallas_call(
        kernel,
        out_shape=(
            jax.ShapeDtypeStruct((LEN, D), BF),
            jax.ShapeDtypeStruct((LEN, D), F32),
            jax.ShapeDtypeStruct((UNITS, 4, 32, D), BF),
            jax.ShapeDtypeStruct((VPAD, 128 if reps == 4 else D), F32),
            jax.ShapeDtypeStruct((1, 1), F32),
        ),
        in_specs=[anywhere, inside, inside, inside, anywhere, anywhere],
        out_specs=(anywhere, anywhere, inside, inside, inside),
        scratch_shapes=[
            pltpu.VMEM((LEN, D), F32),
            pltpu.VMEM((3, 2, D, D), BF),
            pltpu.VMEM((2, nz, 2, 2, 2, 32, D), BF),
            pltpu.VMEM((RC, nz, 2, 2, 32, D), BF),
            pltpu.VMEM((RB, nz, 2, 32, D), BF),
            pltpu.VMEM((UNITS, nz, 32, D), BF),
            pltpu.VMEM((UNITS, nz - 1, 32, D), BF),
            pltpu.VMEM((2, LEN, D), BF),
            pltpu.VMEM((2, LEN, D), BF),
            pltpu.VMEM((LEN, D), F32),
            pltpu.VMEM((FF // D, D), F32),
            pltpu.VMEM((FF // D, D), F32),
            pltpu.VMEM((VPAD, D), F32),
            pltpu.VMEM((8, D), F32),
            pltpu.VMEM((shards, VPAD, 128), F32),
            pltpu.VMEM((reps, VPAD, 128), F32),
            pltpu.VMEM((shards, 8, 128), F32),
            pltpu.SemaphoreType.DMA((UNITS + 1, Reduce.SEMS)),
            pltpu.SemaphoreType.DMA((UNITS, Reduce.SEMS)),
            pltpu.SemaphoreType.DMA((vcount,)),
            pltpu.SemaphoreType.DMA((vcount,)),
            pltpu.SemaphoreType.DMA((3, 2)),
            pltpu.SemaphoreType.DMA((2,)),
        ],
        compiler_params=pltpu.CompilerParams(
            collective_id=1, has_side_effects=True, vmem_limit_bytes=60 * MIB
        ),
        name="back",
    )(tokens, dy, ht, table, act, full)


def norm_kernel(shards, reps, gvec, own, gtable, norm, v1, v2, sq, send, recv):
    vecs = VecSum(shards, reps, gvec, v1, v2, sq, send, recv)
    greet(vecs.row + vecs.col)
    vecs.stage0()
    wide = lax.fori_loop(
        0, own.shape[0], lambda u, acc: acc + fold_squares(own[u]), jnp.zeros((8, D), F32)
    )
    vecs.stage1()
    gtable[...] = vecs.stage2()
    norm[...] = vecs.norm(wide, gtable[...])


def norm_all(gvec, own, shards, reps):
    count = VecSum.sems(shards, reps)

    def kernel(*refs):
        norm_kernel(shards, reps, *refs)

    inside = pl.BlockSpec(memory_space=pltpu.VMEM)
    return pl.pallas_call(
        kernel,
        out_shape=(
            jax.ShapeDtypeStruct((VPAD, 128), F32),
            jax.ShapeDtypeStruct((1, 1), F32),
        ),
        in_specs=[inside, inside],
        out_specs=(inside, inside),
        scratch_shapes=[
            pltpu.VMEM((shards, VPAD, 128), F32),
            pltpu.VMEM((reps, VPAD, 128), F32),
            pltpu.VMEM((shards, 8, 128), F32),
            pltpu.SemaphoreType.DMA((count,)),
            pltpu.SemaphoreType.DMA((count,)),
        ],
        compiler_params=pltpu.CompilerParams(
            collective_id=2, has_side_effects=True, vmem_limit_bytes=56 * MIB
        ),
        name="norm_all",
    )(gvec, own)


def adamw(master, firsts, seconds, gradient, factor, step_rate, decay_amount):
    clipped = gradient * factor
    momentum = 0.9 * firsts + 0.1 * clipped
    variance = 0.95 * seconds + 0.05 * clipped * clipped
    corrected = momentum / (1.0 - 0.9**STEP)
    spread = variance / (1.0 - 0.95**STEP)
    renewed = master - step_rate * (corrected / (jnp.sqrt(spread) + 1e-08) + decay_amount * master)
    return (momentum, variance, renewed)


def update_kernel(shards, norm, own, own_shrink, gtable, *refs):
    ins, passed, outs, through = refs[:15], refs[15:17], refs[17:32], refs[32:34]
    for src, dst in zip(passed, through):
        dst[...] = src[...]
    factor = jnp.minimum(1.0, clip_limit / (norm[...] + 1e-06))
    width = FF // shards

    def part(number, rows, lanes, gradient):
        trio = ins[3 * number : 3 * number + 3]
        new = adamw(
            *(ref[rows, lanes] for ref in trio), gradient.astype(F32), factor, matrix_rate, decay_rate
        )
        for ref, value in zip(outs[3 * number : 3 * number + 3], new):
            ref[rows, lanes] = value

    every = slice(None)
    for i in range(3):
        part(0, every, slice(i * D, i * D + D), own[1 + i])
    part(1, every, every, own[0])
    for j in range(FF // D):
        for s in range(shards):
            f = s * width + j * 128
            part(2, every, slice(f, f + 128), own[5 + 2 * j, :, s * 128 : s * 128 + 128])
    part(3, every, every, own_shrink[0])

    @pl.when(pl.program_id(0) == 0)
    def _():
        new = adamw(*(ref[...] for ref in ins[12:]), gtable[:VROWS], factor, vector_rate, 0.0)
        for ref, value in zip(outs[12:], new):
            ref[...] = value


def update_all(norm, own, gtable, states, passed, shards):
    steps = 4
    moved = [pl.BlockSpec((LEN // steps, D), lambda i: (i, 0))] * 2
    rows = 128 // steps
    per = steps // 4
    specs = []
    for master in states[:12:3]:
        height, lanes = master.shape
        specs += [pl.BlockSpec((height // steps, lanes), lambda i: (i, 0))] * 3

    specs += [pl.BlockSpec((VROWS, 128), lambda i: (0, 0))] * 3

    def kernel(*refs):
        update_kernel(shards, *refs)

    return pl.pallas_call(
        kernel,
        grid=(steps,),
        out_shape=tuple(jax.ShapeDtypeStruct(a.shape, a.dtype) for a in states + passed),
        in_specs=[
            pl.BlockSpec((1, 1), lambda i: (0, 0)),
            pl.BlockSpec((UNITS, rows, D), lambda i: (0, i, 0)),
            pl.BlockSpec((1, 4 * rows, D), lambda i: (4 + 2 * (i // per), i % per, 0)),
            pl.BlockSpec((VPAD, 128), lambda i: (0, 0)),
        ]
        + specs
        + moved,
        out_specs=tuple(specs + moved),
        compiler_params=pltpu.CompilerParams(vmem_limit_bytes=56 * MIB),
        name="update",
    )(norm, own, own, gtable, *states, *passed)


def body(
    tokens,
    doc_lengths,
    cotangent,
    qkv_weight,
    qkv_firsts,
    qkv_seconds,
    dense_weight,
    dense_firsts,
    dense_seconds,
    expand_weight,
    expand_firsts,
    expand_seconds,
    shrink_weight,
    shrink_firsts,
    shrink_seconds,
    vectors,
    vec_firsts,
    vec_seconds,
    *,
    shards,
    reps,
):
    nz = shards // 2
    vec_own = jnp.pad(vectors.astype(BF).T, ((0, VPAD - VROWS), (0, 0)))
    full, table, ht, act = front(
        doc_lengths, tokens, cotangent, qkv_weight, dense_weight, vec_own, expand_weight, shrink_weight, nz
    )
    output, grad_in, owned, gtable, norm = back(
        tokens, cotangent, ht, table, act, full.reshape(UNITS, D, D), nz, reps
    )
    owned = owned.reshape(UNITS, 128, D)
    if reps != 4:
        quads = [[4 * i + j for i in range(reps // 4)] for j in range(4)]
        owned = lax.psum(owned, "rep", axis_index_groups=quads)
        gtable, norm = norm_all(gtable, owned, shards, reps)
    states = (
        qkv_weight, qkv_firsts, qkv_seconds,
        dense_weight, dense_firsts, dense_seconds,
        expand_weight, expand_firsts, expand_seconds,
        shrink_weight, shrink_firsts, shrink_seconds,
        vectors.T, vec_firsts.T, vec_seconds.T,
    )
    new = tuple(update_all(norm, owned, gtable, states, (output, grad_in), shards))
    return new[15:] + new[:12] + tuple(vec.T for vec in new[12:15]) + (norm.reshape(1),)


def solution(mesh):
    shards, reps = mesh.shape["shard"], mesh.shape["rep"]
    data, state = P(("rep", "shard"), None), P("shard", None)

    def step(*args):
        return body(*args, shards=shards, reps=reps)

    return jax.shard_map(
        step,
        mesh=mesh,
        in_specs=(data, data, data) + (state,) * 15,
        out_specs=(data, data) + (state,) * 15 + (P(),),
        check_vma=False,
    )
```

time: 375 us -> 330 us (0.88)
  Pallas kernels: 364 us -> 326 us
  local copies, waits for them, and re-layouts: 5.57 us -> 0.6 us
    pallas_call x1, Pallas kernels: 192 us -> 167 us  [back(): pl.pallas_call(kernel, out_shape=(jax.ShapeDtypeStruct((LEN, D), BF), jax...]
    pallas_call x1, Pallas kernels: 155 us -> 139 us  [front(): pl.pallas_call(kernel, out_shape=(jax.ShapeDtypeStruct((UNITS, nz, 2, 128...]
    unnamed x12 -> x0, local copies, waits for them, and re-layouts: 4.97 us -> none
where the time goes in v2:
time: 330 us; the launch traced here: 329 us
  Pallas kernels  326 us (99%)
    pallas_call x1, Pallas kernels, back(): pl.pallas_call(kernel, out_shape=(jax.ShapeDtypeStruct((LEN, D), BF), jax...  167 us
    pallas_call x1, Pallas kernels, front(): pl.pallas_call(kernel, out_shape=(jax.ShapeDtypeStruct((UNITS, nz, 2, 128...  139 us
    pallas_call x1, Pallas kernels, update_all(): pl.pallas_call(kernel, grid=(steps,), out_shape=tuple((jax.ShapeDtypeStru...  20 us

profile of v2, /device:TPU:0, one launch (start us, length us, event | category | flops | bytes accessed | tf_op | source)
XLA Modules:
  0.0 329.4 jit_solution(8807283793208409897)
XLA Ops:
  0.7 0.7 convert_bitcast_fusion
  1.4 0.6 pad.4.refs_5_
  2.0 139.0 %front.1 = (bf16[12,4,2,128,1024]{4,3,2,1,0:T(8,128)(2,1)}, bf16[16,1024]{1,0:T(8,128)(2,1)}, bf16[1024,1024]{1,0:T(8,128)(2,1)}, bf16[4,1024,1024]{2,1,0:T(8,128)(2,1)}) custom-call(s32[1,4]{1,0:T(1,128)} %refs_0_.2, bf16[1024,1024]{1,0:T(8,128)(2,1)} %refs_0_.3, bf16[1024,1024]{1,0:T(8,128)(2,1)} %refs_1_.3, f32[128,3072]{1,0:T(8,128)} %refs_4_.3, ...), custom_call_target="tpu_custom_call" | custom-call | tf_op jit(solution)/shard_map/front/pallas_call | solution.py:402
  140.9 166.8 %back.1 = (bf16[1024,1024]{1,0:T(8,128)(2,1)}, f32[1024,1024]{1,0:T(8,128)}, bf16[12,4,32,1024]{3,2,1,0:T(8,128)(2,1)}, f32[16,128]{1,0:T(8,128)}, f32[1,1]{1,0:T(1,128)}) custom-call(bf16[1024,1024]{1,0:T(8,128)(2,1)} %refs_0_.3, bf16[1024,1024]{1,0:T(8,128)(2,1)} %refs_1_.3, bf16[1024,1024]{1,0:T(8,128)(2,1)} %get-tuple-element.44.refs_2_, ...), custom_call_target="tpu_custom_call" | custom-call | tf_op jit(solution)/shard_map/back/pallas_call | solution.py:881
  307.7 20.0 %update.1 = (f32[128,3072]{1,0:T(8,128)}, f32[128,3072]{1,0:T(8,128)}, f32[128,3072]{1,0:T(8,128)}, f32[128,1024]{1,0:T(8,128)}, f32[128,1024]{1,0:T(8,128)}, /*...) custom-call(f32[1,1]{1,0:T(1,128)} %get-tuple-element.48.refs_0_, ...), custom_call_target="tpu_custom_call" | custom-call | tf_op jit(solution)/shard_map/update/pallas_call | solution.py:1022

commit v3 on v2

--- a/solution.py
+++ b/solution.py
@@ -151,7 +151,7 @@
     return jnp.concatenate([top, low, u[32:]], axis=0)
 
 
-def heads_attention(base, bias, qt, kt, vt, gt, act, dqt, dkt, dvt, pause):
+def heads_attention(bias, qt, kt, vt, gt, act, dqt, dkt, dvt, pause):
     def scores(head, number):
         q0 = number * QB
         k0 = max(0, number - 2) * QB
@@ -162,14 +162,14 @@
         return q, g, k, v, dot(k, q, 0, 0) + bias[number, :span], dot(v, g, 0, 0)
 
     def weigh(head, number, q, g, k, v, s, dp):
-        outs = pl.ds(pl.multiple_of(base + 64 * head, 64), 64)
+        rows = slice(64 * head, 64 * head + 64)
         e = jnp.exp(s - jnp.max(s, axis=0, keepdims=True))
         p = e * (1.0 / jnp.sum(e, axis=0, keepdims=True))
         pb = p.astype(BF)
         o = dot(v, pb, 1, 0)
         inner = jnp.sum(o * g.astype(F32), axis=0, keepdims=True)
         ds = (p * (dp - inner)).astype(BF)
-        act[0, outs, number * QB : number * QB + QB] = o.astype(BF)
+        act[0, rows, number * QB : number * QB + QB] = o.astype(BF)
         return q, g, k, pb, ds
 
     def spread(head, number, q, g, k, pb, ds):
@@ -201,7 +201,7 @@
 
 JOBS = UNITS + 1
 READY = 6
-LAGS = (0, 2, 3, 5, 6)
+LAGS = (0, 1, 2, 4, 5)
 
 
 def run_stage(gather, stage):
@@ -210,9 +210,9 @@
 
 def front_kernel(
     nz,
-    lengths, tokens, dy, wqkv, wd, vec, wexpand, wshrink,
-    full, table, ht, act,
-    own, expand_f, shrink_f, wd_v, wq_v, bias, cosine, sine, qt, kt, vt, gt, dqf, dkf, dvf,
+    lengths, tokens_hbm, dy_hbm, wqkv, wd, vec, wexpand, wshrink,
+    full, table, ht_hbm, act_hbm,
+    tokens, dy, ht, act, own, expand_f, shrink_f, wd_v, wq_v, bias, cosine, sine, qt, kt, vt, gt, dqf, dkf, dvf,
     send, recv, vsend, vrecv, lsem,
 ):
     at = Place(nz)
@@ -220,8 +220,11 @@
     others = [at.dev(at.r, (at.s + k) % shards) for k in range(1, shards)]
     load_expand = pltpu.make_async_copy(wexpand, expand_f, lsem.at[0])
     load_shrink = pltpu.make_async_copy(wshrink, shrink_f, lsem.at[1])
-    load_expand.start()
-    load_shrink.start()
+    load_tokens = pltpu.make_async_copy(tokens_hbm, tokens, lsem.at[7])
+    load_dy = pltpu.make_async_copy(dy_hbm, dy, lsem.at[8])
+    store_ht = pltpu.make_async_copy(ht, ht_hbm, lsem.at[9])
+    for load in (load_tokens, load_dy, load_expand, load_shrink):
+        load.start()
     own[0] = wd[...].astype(BF)
     for i in range(3):
         own[1 + i] = wqkv[:, i * D : i * D + D].astype(BF)
@@ -320,9 +323,9 @@
     load_dense = pltpu.make_async_copy(full.at[0], wd_v, lsem.at[6])
     side = {
         0: (tables,),
-        1: (wait_vec, lambda: norm_rows(0)),
+        1: (wait_vec, load_tokens.wait, lambda: norm_rows(0)),
         2: (lambda: norm_rows(1), lambda: norm_rows(2)),
-        3: (lambda: norm_rows(3),),
+        3: (lambda: norm_rows(3), store_ht.start),
         4: (cast_rest,),
     }
     for step in range(READY):
@@ -344,6 +347,7 @@
         cols = pl.ds(pl.multiple_of(quad * 256, 256), 256)
         load_quad(quad).wait()
         pl.when(quad == 0)(load_dense.wait)
+        pl.when(quad == 0)(load_dy.wait)
         for part, dst in enumerate((qt, kt, vt)):
             w = wq_v[quad % 2, part].reshape(D, 256)
             u = dot(w, ht[...], 0, 0)
@@ -362,9 +366,14 @@
             w = wd_v[quad, half]
             gt[half * 128 : half * 128 + 128] = dot(w, dy[...], 1, 1).astype(BF)
 
+    def store_act(quad):
+        rows = pl.ds(pl.multiple_of(quad * 256, 256), 256)
+        return pltpu.make_async_copy(act.at[quad % 2], act_hbm.at[:, rows], lsem.at[10 + quad % 2])
+
     def one_quad(quad, carry):
         prepare(quad)
-        base = quad * 256
+        pl.when(quad >= 2)(lambda: store_act(quad - 2).wait())
+        here = act.at[quad % 2]
 
         def pause(number):
             i, left = quad * 4 + number, JOBS + LAGS[-1] - READY
@@ -378,17 +387,20 @@
             if number == 2:
                 pl.when(quad < 3)(lambda: load_quad(quad + 1).start())
 
-        heads_attention(base, bias, qt, kt, vt, gt, act, dqf, dkf, dvf, pause)
+        heads_attention(bias, qt, kt, vt, gt, here, dqf, dkf, dvf, pause)
         for head in range(4):
             rows = slice(64 * head, 64 * head + 64)
-            outs = pl.ds(pl.multiple_of(base + 64 * head, 64), 64)
             back = rotate_rows(dqf[rows], cosine[...], -sine[...]) * (1.0 / math.sqrt(HEAD_DIM))
-            act[1, outs] = back.astype(BF)
-            act[2, outs] = rotate_rows(dkf[rows], cosine[...], -sine[...]).astype(BF)
-            act[3, outs] = dvf[rows].astype(BF)
+            here[1, rows] = back.astype(BF)
+            here[2, rows] = rotate_rows(dkf[rows], cosine[...], -sine[...]).astype(BF)
+            here[3, rows] = dvf[rows].astype(BF)
+        store_act(quad).start()
         return carry
 
     lax.fori_loop(0, 4, one_quad, 0)
+    for quad in (2, 3):
+        store_act(quad).wait()
+    store_ht.wait()
 
 
 def front(lengths, tokens, dy, wqkv, wd, vec, wexpand, wshrink, nz):
@@ -409,16 +421,20 @@
         ),
         in_specs=[
             pl.BlockSpec(memory_space=pltpu.SMEM),
-            inside,
-            inside,
+            anywhere,
+            anywhere,
             inside,
             inside,
             inside,
             anywhere,
             anywhere,
         ],
-        out_specs=(anywhere, inside, inside, inside),
+        out_specs=(anywhere, inside, anywhere, anywhere),
         scratch_shapes=[
+            pltpu.VMEM((LEN, D), BF),
+            pltpu.VMEM((LEN, D), BF),
+            pltpu.VMEM((D, LEN), BF),
+            pltpu.VMEM((2, 4, 256, LEN), BF),
             pltpu.VMEM((UNITS, 128, D), BF),
             pltpu.VMEM(wexpand.shape, F32),
             pltpu.VMEM(wshrink.shape, F32),
@@ -438,7 +454,7 @@
             pltpu.SemaphoreType.DMA((JOBS, 4)),
             pltpu.SemaphoreType.DMA((shards - 1,)),
             pltpu.SemaphoreType.DMA((shards - 1,)),
-            pltpu.SemaphoreType.DMA((8,)),
+            pltpu.SemaphoreType.DMA((12,)),
         ],
         compiler_params=pltpu.CompilerParams(
             collective_id=0, has_side_effects=True, vmem_limit_bytes=58 * MIB
@@ -662,9 +678,9 @@
 
 def back_kernel(
     nz, reps,
-    tokens, dy, ht, table, act, full,
+    tokens, dy_hbm, ht_hbm, table, act, full,
     out_hbm, grad_hbm, owned, gtable, norm,
-    grad_in, wb, grads, rc, rb, ra, rz, gelu, dact, acc, b1, gb1, gv, wide, v1, v2, sq,
+    dy, ht, grad_in, wb, grads, rc, rb, ra, rz, gelu, dact, acc, b1, gb1, gv, wide, v1, v2, sq,
     send, recv, vsend, vrecv, wsem, osem,
 ):
     at = Place(nz)
@@ -683,7 +699,11 @@
     def load_mlp(j):
         load((j + 2) % 3, full.at[4 + 2 * j], full.at[5 + 2 * j])
 
+    load_dy = pltpu.make_async_copy(dy_hbm, dy, osem.at[2])
+    load_ht = pltpu.make_async_copy(ht_hbm, ht, osem.at[3])
+    load_dy.start()
     load(0, act.at[0], full.at[0])
+    load_ht.start()
     load(2, full.at[4], full.at[5])
     load(1, act.at[1], full.at[1])
     out = wb.at[0, 1]
@@ -772,18 +792,20 @@
         dense, qkv = t == 0, (t >= 1) & (t < 4)
         even, odd = t % 2 == 0, t % 2 == 1
         shrink, expand = (t >= 4) & (t < UNITS) & even, (t >= 4) & (t < UNITS) & odd
-        again = (t >= 8) & (t < 11)
+        again = (t >= 9) & (t < 12)
         slot = t % 2
         j = (t - 4) // 2
 
         pl.when(t < 4)(lambda: loaded(slot))
+        pl.when(t == 0)(load_dy.wait)
+        pl.when(t == 1)(load_ht.wait)
         pl.when(t == 1)(lambda: loaded(2))
         pl.when((t == 1) | (t == 2))(lambda: load(1 - slot, act.at[t + 1], full.at[t + 1]))
         pl.when((t == 3) | (t == 4))(lambda: load_mlp(t - 2))
         pl.when(t == 6)(lambda: load_mlp(3))
-        pl.when(again)(lambda: load(0, act.at[t - 7], full.at[t - 7]))
+        pl.when(again)(lambda: load(0, act.at[t - 8], full.at[t - 8]))
         inputs = pltpu.make_async_copy(tokens, wb.at[0, 0], wsem.at[0, 0])
-        pl.when(t == 11)(lambda: inputs.start())
+        pl.when(t == 12)(lambda: inputs.start())
 
         pl.when(dense)(
             lambda: tiles(lambda n: write(t, n, dot(wb[slot, 0], dy[:, cols(n)], 1, 0)))
@@ -837,7 +859,7 @@
 
             def tile(n):
                 grad_in[:, cols(n)] += dot(wb[0, 0], wb[0, 1, cols(n), :], 0, 1)
-                gv[pl.ds(t - 6, 1), cols(n)] = dot(ones, wb[0, 0, cols(n), :], 1, 1)[:1]
+                gv[pl.ds(t - 7, 1), cols(n)] = dot(ones, wb[0, 0, cols(n), :], 1, 1)[:1]
 
             tiles(tile)
 
@@ -887,9 +909,11 @@
             jax.ShapeDtypeStruct((VPAD, 128 if reps == 4 else D), F32),
             jax.ShapeDtypeStruct((1, 1), F32),
         ),
-        in_specs=[anywhere, inside, inside, inside, anywhere, anywhere],
+        in_specs=[anywhere, anywhere, anywhere, inside, anywhere, anywhere],
         out_specs=(anywhere, anywhere, inside, inside, inside),
         scratch_shapes=[
+            pltpu.VMEM((LEN, D), BF),
+            pltpu.VMEM((D, LEN), BF),
             pltpu.VMEM((LEN, D), F32),
             pltpu.VMEM((3, 2, D, D), BF),
             pltpu.VMEM((2, nz, 2, 2, 2, 32, D), BF),
@@ -912,7 +936,7 @@
             pltpu.SemaphoreType.DMA((vcount,)),
             pltpu.SemaphoreType.DMA((vcount,)),
             pltpu.SemaphoreType.DMA((3, 2)),
-            pltpu.SemaphoreType.DMA((2,)),
+            pltpu.SemaphoreType.DMA((4,)),
         ],
         compiler_params=pltpu.CompilerParams(
             collective_id=1, has_side_effects=True, vmem_limit_bytes=60 * MIB
@@ -972,69 +996,88 @@
     return (momentum, variance, renewed)
 
 
-def update_kernel(shards, norm, own, own_shrink, gtable, *refs):
-    ins, passed, outs, through = refs[:15], refs[15:17], refs[17:32], refs[32:34]
-    for src, dst in zip(passed, through):
-        dst[...] = src[...]
+def update_kernel(shards, norm, own, gtable, *refs):
+    ins, outs, bufs, sin, sout = refs[:17], refs[17:34], refs[34:51], refs[51], refs[52]
+    loads = [pltpu.make_async_copy(ins[i], bufs[i], sin.at[i]) for i in range(17)]
+    stores = [pltpu.make_async_copy(bufs[i], outs[i], sout.at[i]) for i in range(17)]
     factor = jnp.minimum(1.0, clip_limit / (norm[...] + 1e-06))
     width = FF // shards
-
-    def part(number, rows, lanes, gradient):
-        trio = ins[3 * number : 3 * number + 3]
-        new = adamw(
-            *(ref[rows, lanes] for ref in trio), gradient.astype(F32), factor, matrix_rate, decay_rate
-        )
-        for ref, value in zip(outs[3 * number : 3 * number + 3], new):
+    order = (2, 3, 0, 1, 4)
+    for number in order:
+        for i in range(3 * number, 3 * number + 3):
+            loads[i].start()
+    for i in (15, 16):
+        loads[i].start()
+
+    def part(number, rows, lanes, gradient, rate=matrix_rate, decay=decay_rate):
+        trio = bufs[3 * number : 3 * number + 3]
+        new = adamw(*(ref[rows, lanes] for ref in trio), gradient.astype(F32), factor, rate, decay)
+        for ref, value in zip((trio[1], trio[2], trio[0]), new):
             ref[rows, lanes] = value
 
-    every = slice(None)
-    for i in range(3):
-        part(0, every, slice(i * D, i * D + D), own[1 + i])
-    part(1, every, every, own[0])
-    for j in range(FF // D):
-        for s in range(shards):
-            f = s * width + j * 128
-            part(2, every, slice(f, f + 128), own[5 + 2 * j, :, s * 128 : s * 128 + 128])
-    part(3, every, every, own_shrink[0])
-
-    @pl.when(pl.program_id(0) == 0)
-    def _():
-        new = adamw(*(ref[...] for ref in ins[12:]), gtable[:VROWS], factor, vector_rate, 0.0)
-        for ref, value in zip(outs[12:], new):
-            ref[...] = value
+    def expand(rows):
+        for j in range(FF // D):
+            for s in range(shards):
+                f = s * width + j * 128
+                part(2, rows, slice(f, f + 128), own[5 + 2 * j, rows, s * 128 : s * 128 + 128])
+
+    def shrink(rows):
+        for j in range(FF // D):
+            there = pl.ds(pl.multiple_of(j * 128 + rows.start, 16), rows.size)
+            part(3, there, slice(None), own[4 + 2 * j, rows])
+
+    def qkv(rows):
+        for i in range(3):
+            part(0, rows, slice(i * D, i * D + D), own[1 + i, rows])
+
+    def dense(rows):
+        part(1, rows, slice(None), own[0, rows])
+
+    def vectors(rows):
+        part(4, slice(None), slice(None), gtable[:VROWS], vector_rate, 0.0)
+
+    for number in order:
+        for i in range(3 * number, 3 * number + 3):
+            loads[i].wait()
+        work = (qkv, dense, expand, shrink, vectors)[number]
+        if number == 4:
+            work(None)
+        else:
+
+            def some(i, carry, work=work):
+                work(pl.ds(pl.multiple_of(i * 16, 16), 16))
+                return carry
+
+            lax.fori_loop(0, 8, some, 0)
+        for i in range(3 * number, 3 * number + 3):
+            stores[i].start()
+    for i in (15, 16):
+        loads[i].wait()
+        stores[i].start()
+    for store in stores:
+        store.wait()
 
 
 def update_all(norm, own, gtable, states, passed, shards):
-    steps = 4
-    moved = [pl.BlockSpec((LEN // steps, D), lambda i: (i, 0))] * 2
-    rows = 128 // steps
-    per = steps // 4
-    specs = []
-    for master in states[:12:3]:
-        height, lanes = master.shape
-        specs += [pl.BlockSpec((height // steps, lanes), lambda i: (i, 0))] * 3
-
-    specs += [pl.BlockSpec((VROWS, 128), lambda i: (0, 0))] * 3
+    arrays = states + passed
+    anywhere = [pl.BlockSpec(memory_space=pl.ANY)] * len(arrays)
+    inside = [pl.BlockSpec(memory_space=pltpu.VMEM)] * 3
 
     def kernel(*refs):
         update_kernel(shards, *refs)
 
-    return pl.pallas_call(
+    new = pl.pallas_call(
         kernel,
-        grid=(steps,),
-        out_shape=tuple(jax.ShapeDtypeStruct(a.shape, a.dtype) for a in states + passed),
-        in_specs=[
-            pl.BlockSpec((1, 1), lambda i: (0, 0)),
-            pl.BlockSpec((UNITS, rows, D), lambda i: (0, i, 0)),
-            pl.BlockSpec((1, 4 * rows, D), lambda i: (4 + 2 * (i // per), i % per, 0)),
-            pl.BlockSpec((VPAD, 128), lambda i: (0, 0)),
-        ]
-        + specs
-        + moved,
-        out_specs=tuple(specs + moved),
+        out_shape=tuple(jax.ShapeDtypeStruct(a.shape, a.dtype) for a in arrays),
+        in_specs=inside + anywhere,
+        out_specs=tuple(anywhere),
+        scratch_shapes=[pltpu.VMEM(a.shape, a.dtype) for a in arrays]
+        + [pltpu.SemaphoreType.DMA((len(arrays),)), pltpu.SemaphoreType.DMA((len(arrays),))],
         compiler_params=pltpu.CompilerParams(vmem_limit_bytes=56 * MIB),
         name="update",
-    )(norm, own, own, gtable, *states, *passed)
+    )(norm, own, gtable, *arrays)
+    ordered = [new[3 * i + k] for i in range(5) for k in (1, 2, 0)]
+    return ordered + list(new[15:])
 
 
 def body(

time: 330 us -> 318 us (0.964)
  Pallas kernels: 326 us -> 314 us
    pallas_call x1, Pallas kernels: 139 us -> 131 us  [front(): pl.pallas_call(kernel, out_shape=(jax.ShapeDtypeStruct((UNITS, nz, 2, 128...]
where the time goes in v3:
time: 318 us
  Pallas kernels  314 us (99%)
    pallas_call x1, Pallas kernels, back(): pl.pallas_call(kernel, out_shape=(jax.ShapeDtypeStruct((LEN, D), BF), jax...  164 us
    pallas_call x1, Pallas kernels, front(): pl.pallas_call(kernel, out_shape=(jax.ShapeDtypeStruct((UNITS, nz, 2, 128...  131 us
    pallas_call x1, Pallas kernels, update_all(): pl.pallas_call(kernel, out_shape=tuple((jax.ShapeDtypeStruct(a.shape, a.d...  18.2 us

profile of v3, /device:TPU:0, one launch (start us, length us, event | category | flops | bytes accessed | tf_op | source)
XLA Modules:
  0.0 317.8 jit_solution(3418776480087322452)
XLA Ops:
  0.7 0.7 convert_bitcast_fusion
  1.4 0.6 pad.4.refs_5_
  2.0 131.5 %front.1 = (bf16[12,4,2,128,1024]{4,3,2,1,0:T(8,128)(2,1)}, bf16[16,1024]{1,0:T(8,128)(2,1)}, bf16[1024,1024]{1,0:T(8,128)(2,1)}, bf16[4,1024,1024]{2,1,0:T(8,128)(2,1)}) custom-call(s32[1,4]{1,0:T(1,128)} %refs_0_.2, bf16[1024,1024]{1,0:T(8,128)(2,1)} %refs_0_.3, bf16[1024,1024]{1,0:T(8,128)(2,1)} %refs_1_.3, f32[128,3072]{1,0:T(8,128)} %refs_3_.3, ...), custom_call_target="tpu_custom_call" | custom-call | tf_op jit(solution)/shard_map/front/pallas_call | solution.py:414
  133.4 164.5 %back.1 = (bf16[1024,1024]{1,0:T(8,128)(2,1)}, f32[1024,1024]{1,0:T(8,128)}, bf16[12,4,32,1024]{3,2,1,0:T(8,128)(2,1)}, f32[16,128]{1,0:T(8,128)}, f32[1,1]{1,0:T(1,128)}) custom-call(bf16[1024,1024]{1,0:T(8,128)(2,1)} %refs_0_.3, bf16[1024,1024]{1,0:T(8,128)(2,1)} %refs_1_.3, bf16[1024,1024]{1,0:T(8,128)(2,1)} %get-tuple-element.44.refs_2_, ...), custom_call_target="tpu_custom_call" | custom-call | tf_op jit(solution)/shard_map/back/pallas_call | solution.py:903
  297.9 18.2 %update.1 = (f32[128,3072]{1,0:T(8,128)}, f32[128,3072]{1,0:T(8,128)}, f32[128,3072]{1,0:T(8,128)}, f32[128,1024]{1,0:T(8,128)}, f32[128,1024]{1,0:T(8,128)}, /*...) custom-call(f32[1,1]{1,0:T(1,128)} %get-tuple-element.48.refs_0_, ...), custom_call_target="tpu_custom_call" | custom-call | tf_op jit(solution)/shard_map/update/pallas_call | solution.py:1069

commit v4 on v3

--- a/solution.py
+++ b/solution.py
@@ -73,11 +73,19 @@
         )
 
 
-def greet(peers):
+def hail(peers):
     barrier = pltpu.get_barrier_semaphore()
     for peer in peers:
         pl.semaphore_signal(barrier, inc=1, device_id=peer, device_id_type=pl.DeviceIdType.MESH)
-    pl.semaphore_wait(barrier, len(peers))
+
+
+def hear(peers):
+    pl.semaphore_wait(pltpu.get_barrier_semaphore(), len(peers))
+
+
+def greet(peers):
+    hail(peers)
+    hear(peers)
 
 
 def remote(src, dst, send, recv, peer):
@@ -211,13 +219,14 @@
 def front_kernel(
     nz,
     lengths, tokens_hbm, dy_hbm, wqkv, wd, vec, wexpand, wshrink,
-    full, table, ht_hbm, act_hbm,
-    tokens, dy, ht, act, own, expand_f, shrink_f, wd_v, wq_v, bias, cosine, sine, qt, kt, vt, gt, dqf, dkf, dvf,
+    full, table, ht_hbm, act_hbm, grads_hbm,
+    tokens, dy, ht, act, gqkv, gdense, own, expand_f, shrink_f, wd_v, wq_v, bias, cosine, sine, qt, kt, vt, gt, dqf, dkf, dvf,
     send, recv, vsend, vrecv, lsem,
 ):
     at = Place(nz)
     shards = 2 * nz
     others = [at.dev(at.r, (at.s + k) % shards) for k in range(1, shards)]
+    hail(others + [at.ypeer, at.cpeer])
     load_expand = pltpu.make_async_copy(wexpand, expand_f, lsem.at[0])
     load_shrink = pltpu.make_async_copy(wshrink, shrink_f, lsem.at[1])
     load_tokens = pltpu.make_async_copy(tokens_hbm, tokens, lsem.at[7])
@@ -228,7 +237,7 @@
     own[0] = wd[...].astype(BF)
     for i in range(3):
         own[1 + i] = wqkv[:, i * D : i * D + D].astype(BF)
-    greet(others + [at.ypeer, at.cpeer])
+    hear(others + [at.ypeer, at.cpeer])
 
     def lanes(i):
         return pl.ds(pl.multiple_of(i * 128, 128), 128)
@@ -370,19 +379,30 @@
         rows = pl.ds(pl.multiple_of(quad * 256, 256), 256)
         return pltpu.make_async_copy(act.at[quad % 2], act_hbm.at[:, rows], lsem.at[10 + quad % 2])
 
+    def store_grads(quad):
+        part = pl.ds(pl.multiple_of(quad * 256, 256), 256)
+        slot = quad % 2
+        return (
+            pltpu.make_async_copy(
+                gqkv.at[slot], grads_hbm.at[pl.ds(1, 3), :, part], lsem.at[12 + slot]
+            ),
+            pltpu.make_async_copy(gdense.at[slot], grads_hbm.at[0, part], lsem.at[14 + slot]),
+        )
+
+    def stored(quad):
+        store_act(quad).wait()
+        for copy in store_grads(quad):
+            copy.wait()
+
     def one_quad(quad, carry):
         prepare(quad)
-        pl.when(quad >= 2)(lambda: store_act(quad - 2).wait())
+        pl.when(quad >= 2)(lambda: stored(quad - 2))
         here = act.at[quad % 2]
 
         def pause(number):
-            i, left = quad * 4 + number, JOBS + LAGS[-1] - READY
-            before, after = ((n * left + HEADS - 1) // HEADS for n in (i, i + 1))
-
-            @pl.when(after > before)
-            def _():
+            if number != 1:
                 for stage, lag in enumerate(LAGS):
-                    part(READY + before - lag, stage)
+                    part(READY + 3 * quad + max(0, number - 1) - lag, stage)
 
             if number == 2:
                 pl.when(quad < 3)(lambda: load_quad(quad + 1).start())
@@ -395,11 +415,16 @@
             here[2, rows] = rotate_rows(dkf[rows], cosine[...], -sine[...]).astype(BF)
             here[3, rows] = dvf[rows].astype(BF)
         store_act(quad).start()
+        for i in range(3):
+            gqkv[quad % 2, i] = dot(ht[...], here[1 + i], 1, 1).astype(BF)
+        gdense[quad % 2] = dot(here[0], dy[...], 1, 0).astype(BF)
+        for copy in store_grads(quad):
+            copy.start()
         return carry
 
     lax.fori_loop(0, 4, one_quad, 0)
     for quad in (2, 3):
-        store_act(quad).wait()
+        stored(quad)
     store_ht.wait()
 
 
@@ -418,6 +443,7 @@
             jax.ShapeDtypeStruct((VPAD, D), BF),
             jax.ShapeDtypeStruct((D, LEN), BF),
             jax.ShapeDtypeStruct((4, D, LEN), BF),
+            jax.ShapeDtypeStruct((4, D, D), BF),
         ),
         in_specs=[
             pl.BlockSpec(memory_space=pltpu.SMEM),
@@ -429,12 +455,14 @@
             anywhere,
             anywhere,
         ],
-        out_specs=(anywhere, inside, anywhere, anywhere),
+        out_specs=(anywhere, inside, anywhere, anywhere, anywhere),
         scratch_shapes=[
             pltpu.VMEM((LEN, D), BF),
             pltpu.VMEM((LEN, D), BF),
             pltpu.VMEM((D, LEN), BF),
             pltpu.VMEM((2, 4, 256, LEN), BF),
+            pltpu.VMEM((2, 3, D, 256), BF),
+            pltpu.VMEM((2, 256, D), BF),
             pltpu.VMEM((UNITS, 128, D), BF),
             pltpu.VMEM(wexpand.shape, F32),
             pltpu.VMEM(wshrink.shape, F32),
@@ -454,7 +482,7 @@
             pltpu.SemaphoreType.DMA((JOBS, 4)),
             pltpu.SemaphoreType.DMA((shards - 1,)),
             pltpu.SemaphoreType.DMA((shards - 1,)),
-            pltpu.SemaphoreType.DMA((12,)),
+            pltpu.SemaphoreType.DMA((16,)),
         ],
         compiler_params=pltpu.CompilerParams(
             collective_id=0, has_side_effects=True, vmem_limit_bytes=58 * MIB
@@ -534,6 +562,7 @@
         at = self.at
         self.c(u).wait_recv()
         add_into(self.rc.at[u % RC], self.grads.at[u % 2, :, :, at.c])
+        self.c(u).wait_send()
         self.either(u, lambda on_x: self.b(u, on_x).start())
 
     def phase2(self, u):
@@ -547,7 +576,6 @@
 
         self.either(u, add)
         self.b(u, True).wait_send()
-        self.c(u).wait_send()
 
     def phase3(self, u):
         at = self.at
@@ -678,10 +706,10 @@
 
 def back_kernel(
     nz, reps,
-    tokens, dy_hbm, ht_hbm, table, act, full,
+    tokens, dy_hbm, ht_hbm, table, act, full, ready,
     out_hbm, grad_hbm, owned, gtable, norm,
     dy, ht, grad_in, wb, grads, rc, rb, ra, rz, gelu, dact, acc, b1, gb1, gv, wide, v1, v2, sq,
-    send, recv, vsend, vrecv, wsem, osem,
+    send, recv, vsend, vrecv, wsem, osem, gsem,
 ):
     at = Place(nz)
     shards = 2 * nz
@@ -701,26 +729,36 @@
 
     load_dy = pltpu.make_async_copy(dy_hbm, dy, osem.at[2])
     load_ht = pltpu.make_async_copy(ht_hbm, ht, osem.at[3])
+    vecs = VecSum(shards, reps, gv, v1, v2, sq, vsend, vrecv)
+    peers = vecs.row + [at.ypeer, at.cpeer, at.diag]
+    hail(peers)
+
+    def load_grad(u):
+        return pltpu.make_async_copy(ready.at[u], grads.at[u % 2], gsem.at[u % 2])
+
+    load_grad(0).start()
+    load_grad(1).start()
     load_dy.start()
-    load(0, act.at[0], full.at[0])
     load_ht.start()
-    load(2, full.at[4], full.at[5])
-    load(1, act.at[1], full.at[1])
+    for j in range(3):
+        load_mlp(j)
     out = wb.at[0, 1]
     out_copy = pltpu.make_async_copy(out, out_hbm, osem.at[0])
     grad_copy = pltpu.make_async_copy(grad_in, grad_hbm, osem.at[1])
     red = Reduce(at, grads, rc, rb, ra, rz, owned, send, recv)
-    vecs = VecSum(shards, reps, gv, v1, v2, sq, vsend, vrecv)
-    gv[...] = jnp.zeros((VPAD, D), F32)
-    wide[...] = jnp.zeros((8, D), F32)
-    grad_in[...] = jnp.zeros((LEN, D), F32)
-    for j in range(FF // D):
-        for s in range(shards):
-            f = s * width + j * 128
-            b1[j : j + 1, s * 128 : s * 128 + 128] = table[
-                6 + f // D : 7 + f // D, f % D : f % D + 128
-            ].astype(F32)
-    greet(vecs.row + [at.ypeer, at.cpeer, at.diag])
+    hear(peers)
+
+    def prepare():
+        gv[...] = jnp.zeros((VPAD, D), F32)
+        wide[...] = jnp.zeros((8, D), F32)
+        grad_in[...] = jnp.zeros((LEN, D), F32)
+        acc[...] = jnp.zeros((LEN, D), F32)
+        for j in range(FF // D):
+            for s in range(shards):
+                f = s * width + j * 128
+                b1[j : j + 1, s * 128 : s * 128 + 128] = table[
+                    6 + f // D : 7 + f // D, f % D : f % D + 128
+                ].astype(F32)
 
     def write(u, n, value):
         grads[u % 2, :, :, :, :, :, cols(n)] = value.astype(BF).reshape(nz, 2, 2, 2, 32, WIDE)
@@ -789,30 +827,18 @@
 
             pl.when((u >= 0) & (u < UNITS))(phase)
 
-        dense, qkv = t == 0, (t >= 1) & (t < 4)
         even, odd = t % 2 == 0, t % 2 == 1
         shrink, expand = (t >= 4) & (t < UNITS) & even, (t >= 4) & (t < UNITS) & odd
-        again = (t >= 9) & (t < 12)
-        slot = t % 2
+        again = (t >= 8) & (t < UNITS)
         j = (t - 4) // 2
 
-        pl.when(t < 4)(lambda: loaded(slot))
-        pl.when(t == 0)(load_dy.wait)
-        pl.when(t == 1)(load_ht.wait)
-        pl.when(t == 1)(lambda: loaded(2))
-        pl.when((t == 1) | (t == 2))(lambda: load(1 - slot, act.at[t + 1], full.at[t + 1]))
-        pl.when((t == 3) | (t == 4))(lambda: load_mlp(t - 2))
+        pl.when((t == 1) | (t == 2))(lambda: load_grad(t + 1).start())
         pl.when(t == 6)(lambda: load_mlp(3))
         pl.when(again)(lambda: load(0, act.at[t - 8], full.at[t - 8]))
         inputs = pltpu.make_async_copy(tokens, wb.at[0, 0], wsem.at[0, 0])
         pl.when(t == 12)(lambda: inputs.start())
 
-        pl.when(dense)(
-            lambda: tiles(lambda n: write(t, n, dot(wb[slot, 0], dy[:, cols(n)], 1, 0)))
-        )
-        pl.when(qkv)(
-            lambda: tiles(lambda n: write(t, n, dot(ht[...], wb[slot, 0, cols(n), :], 1, 1)))
-        )
+        pl.when(t < 4)(lambda: load_grad(t).wait())
         pl.when(shrink)(
             lambda: tiles(lambda n: write(t, n, dot(gelu[j % 2], dy[:, cols(n)], 0, 0)))
         )
@@ -822,29 +848,26 @@
             )
         )
         pl.when(t < UNITS)(lambda: red.phase0(t))
-
-        @pl.when(dense)
+        pl.when(t == 0)(prepare)
+
+        @pl.when(t == 1)
+        def _():
+            load_dy.wait()
+            load_ht.wait()
+            loaded(2)
+
+        @pl.when(shrink)
         def _():
             def tile(n):
-                acc[:, cols(n)] = dot(wb[slot, 0], wb[slot, 1, :, cols(n)], 0, 0)
+                acc[:, cols(n)] += dot(gelu[j % 2], wb[(j + 2) % 3, 0, :, cols(n)], 1, 0)
 
             tiles(tile)
 
-        ends = (t == UNITS) | (t == UNITS + 1)
-        of = jnp.where(ends, t - UNITS + 2, j)
-
-        @pl.when((shrink & (t < 8)) | ends)
-        def _():
-            def tile(n):
-                acc[:, cols(n)] += dot(gelu[of % 2], wb[(of + 2) % 3, 0, :, cols(n)], 1, 0)
-
-            tiles(tile)
-
-        @pl.when((expand & (t < 8)) | ends)
+        @pl.when(expand)
         def _():
             def tile(n):
                 grad_in[:, cols(n)] += dot(
-                    dact[of % 2], wb[(of + 2) % 3, 1, cols(n), :], 1, 1
+                    dact[j % 2], wb[(j + 2) % 3, 1, cols(n), :], 1, 1
                 )
 
             tiles(tile)
@@ -852,9 +875,17 @@
         pl.when((t == 3) | (t == 5) | (t == 7))(lambda: loaded((t // 2 + 2) % 3))
         pl.when((t >= 1) & (t < 9))(lambda: activate((t - 1) // 2, 1 - t % 2))
 
-        @pl.when(again)
+        pl.when(again)(lambda: loaded(0))
+
+        @pl.when(t == 8)
         def _():
-            loaded(0)
+            def tile(n):
+                acc[:, cols(n)] += dot(wb[0, 0], wb[0, 1, :, cols(n)], 0, 0)
+
+            tiles(tile)
+
+        @pl.when(again & (t > 8))
+        def _():
             ones = jnp.ones((8, LEN), BF)
 
             def tile(n):
@@ -863,7 +894,7 @@
 
             tiles(tile)
 
-        @pl.when(t == UNITS + 2)
+        @pl.when(t == UNITS + 1)
         def _():
             inputs.wait()
             finish()
@@ -871,10 +902,10 @@
             grad_copy.start()
 
         if fused:
-            pl.when(t == UNITS + 3)(vecs.stage0)
-            pl.when(t == UNITS + 4)(vecs.stage1)
-
-            @pl.when(t == UNITS + 5)
+            pl.when(t == UNITS + 2)(vecs.stage0)
+            pl.when(t == UNITS + 3)(vecs.stage1)
+
+            @pl.when(t == UNITS + 4)
             def _():
                 gtable[...] = vecs.stage2()
 
@@ -891,7 +922,7 @@
         norm[...] = jnp.zeros((1, 1), F32)
 
 
-def back(tokens, dy, ht, table, act, full, nz, reps):
+def back(tokens, dy, ht, table, act, full, ready, nz, reps):
     shards = 2 * nz
     vcount = VecSum.sems(shards, reps)
     anywhere = pl.BlockSpec(memory_space=pl.ANY)
@@ -909,7 +940,7 @@
             jax.ShapeDtypeStruct((VPAD, 128 if reps == 4 else D), F32),
             jax.ShapeDtypeStruct((1, 1), F32),
         ),
-        in_specs=[anywhere, anywhere, anywhere, inside, anywhere, anywhere],
+        in_specs=[anywhere, anywhere, anywhere, inside, anywhere, anywhere, anywhere],
         out_specs=(anywhere, anywhere, inside, inside, inside),
         scratch_shapes=[
             pltpu.VMEM((LEN, D), BF),
@@ -937,12 +968,13 @@
             pltpu.SemaphoreType.DMA((vcount,)),
             pltpu.SemaphoreType.DMA((3, 2)),
             pltpu.SemaphoreType.DMA((4,)),
+            pltpu.SemaphoreType.DMA((2,)),
         ],
         compiler_params=pltpu.CompilerParams(
             collective_id=1, has_side_effects=True, vmem_limit_bytes=60 * MIB
         ),
         name="back",
-    )(tokens, dy, ht, table, act, full)
+    )(tokens, dy, ht, table, act, full, ready)
 
 
 def norm_kernel(shards, reps, gvec, own, gtable, norm, v1, v2, sq, send, recv):
@@ -1105,11 +1137,12 @@
 ):
     nz = shards // 2
     vec_own = jnp.pad(vectors.astype(BF).T, ((0, VPAD - VROWS), (0, 0)))
-    full, table, ht, act = front(
+    full, table, ht, act, ready = front(
         doc_lengths, tokens, cotangent, qkv_weight, dense_weight, vec_own, expand_weight, shrink_weight, nz
     )
     output, grad_in, owned, gtable, norm = back(
-        tokens, cotangent, ht, table, act, full.reshape(UNITS, D, D), nz, reps
+        tokens, cotangent, ht, table, act, full.reshape(UNITS, D, D),
+        ready.reshape(4, nz, 2, 2, 2, 32, D), nz, reps,
     )
     owned = owned.reshape(UNITS, 128, D)
     if reps != 4:

time: 318 us -> 315 us (level)
  no operation moved by 1% of the time
where the time goes in v4:
time: 315 us
  Pallas kernels  311 us (99%)
    pallas_call x1, Pallas kernels, back(): pl.pallas_call(kernel, out_shape=(jax.ShapeDtypeStruct((LEN, D), BF), jax...  162 us
    pallas_call x1, Pallas kernels, front(): pl.pallas_call(kernel, out_shape=(jax.ShapeDtypeStruct((UNITS, nz, 2, 128...  131 us
    pallas_call x1, Pallas kernels, update_all(): pl.pallas_call(kernel, out_shape=tuple((jax.ShapeDtypeStruct(a.shape, a.d...  18.2 us

profile of v4, /device:TPU:0, one launch (start us, length us, event | category | flops | bytes accessed | tf_op | source)
XLA Modules:
  0.0 314.7 jit_solution(14836269467227926968)
XLA Ops:
  0.7 0.7 convert_bitcast_fusion
  1.4 0.6 pad.4.refs_5_
  2.0 130.6 %front.1 = (bf16[12,4,2,128,1024]{4,3,2,1,0:T(8,128)(2,1)}, bf16[16,1024]{1,0:T(8,128)(2,1)}, bf16[1024,1024]{1,0:T(8,128)(2,1)}, bf16[4,1024,1024]{2,1,0:T(8,128)(2,1)}, bf16[4,1024,1024]{2,1,0:T(8,128)(2,1)}) custom-call(s32[1,4]{1,0:T(1,128)} %refs_0_.2, bf16[1024,1024]{1,0:T(8,128)(2,1)} %refs_0_.3, bf16[1024,1024]{1,0:T(8,128)(2,1)} %refs_1_.3, ...), custom_call_target="tpu_custom_call" | custom-call | tf_op jit(solution)/shard_map/front/pallas_call | solution.py:439
  132.5 162.1 %back.1 = (bf16[1024,1024]{1,0:T(8,128)(2,1)}, f32[1024,1024]{1,0:T(8,128)}, bf16[12,4,32,1024]{3,2,1,0:T(8,128)(2,1)}, f32[16,128]{1,0:T(8,128)}, f32[1,1]{1,0:T(1,128)}) custom-call(bf16[1024,1024]{1,0:T(8,128)(2,1)} %refs_0_.3, bf16[1024,1024]{1,0:T(8,128)(2,1)} %refs_1_.3, bf16[1024,1024]{1,0:T(8,128)(2,1)} %get-tuple-element.45.refs_2_, ...), custom_call_target="tpu_custom_call" | custom-call | tf_op jit(solution)/shard_map/back/pallas_call | solution.py:934
  294.7 18.2 %update.1 = (f32[128,3072]{1,0:T(8,128)}, f32[128,3072]{1,0:T(8,128)}, f32[128,3072]{1,0:T(8,128)}, f32[128,1024]{1,0:T(8,128)}, f32[128,1024]{1,0:T(8,128)}, /*...) custom-call(f32[1,1]{1,0:T(1,128)} %get-tuple-element.50.refs_0_, ...), custom_call_target="tpu_custom_call" | custom-call | tf_op jit(solution)/shard_map/update/pallas_call | solution.py:1101
